TPU v7x, 128 devices: a whole 4x4x4 slice. The times are simulated.
128 devices in a mesh: pt: 32 (over x, y, core), var: 4 (over z).
Axes of the slice: x: 4, y: 4, z: 4, core: 2. Of those that a mesh axis runs over, the one named last changes fastest.
Arguments:
- green_tensor: bfloat16 [6, 2, 1024, 1024], P(None, None, ('pt', 'var')), may hold values from -0.0078125 to 0.0078125
- moment: bfloat16 [6, 1024], P(None, ('pt', 'var')), may hold values from -6 to 6
- slip_rate: bfloat16 [64, 1024, 1024], P('var', 'pt'), may hold values from -6 to 6
- owner_shard: int32 [1024, 1], P('pt'), may hold values from 0 to 31; in each aligned block of 32 rows (0 to 31, 32 to 63, ...) at most 2 rows name the same one
- point_slot: int32 [1024], P('pt'), may hold values from 0 to 31
- live_counts: int32 [32], P('pt'), may hold values from 1 to 32, 768 in all
Outputs:
- seismograms: float32 [64, 2, 1024], P('var', None, 'pt')
Inputs may be any that keep to these rules, and one draw needn't show every extreme that they name: `owner_shard`: within each aligned block of 32 rows (the rows of one index of pt), no value is named by more than 2 rows; some block names one value exactly 2 times. `live_counts`: the counts sum to 768 and one of them equals 32.
All inputs are finite; a program needn't handle non-finite values. No bound on the sum of `live_counts` on one device may be relied on, other than what follows from the above.
Results may differ from a plain program's by a relative error of at most 0.0029.
Values may be sent and summed in bfloat16 or wider, within the bound.
A program may use at most 256 MiB of HBM per device.

v0:
```python
import jax
import jax.numpy as jnp
from jax import lax
from jax.sharding import PartitionSpec as P


def combine(green_tensor, moment):
    return jnp.sum(
        moment.astype(jnp.float32)[:, None, :, None] * green_tensor.astype(jnp.float32), axis=0
    ).astype(jnp.bfloat16)


def lag_tiles(rows_green, tile_width):
    count_rows = rows_green.shape[1]
    length = rows_green.shape[2]
    blocks = length // tile_width
    padded = jnp.pad(rows_green, ((0, 0), (0, 0), (tile_width, 0)))
    framed = padded.reshape(2, count_rows, blocks + 1, tile_width)
    windows = jnp.concatenate([framed[:, :, :blocks, :], framed[:, :, 1:, :]], axis=-1)
    windows = jnp.transpose(windows, (2, 0, 1, 3))
    row_index = jnp.arange(tile_width, dtype=jnp.int32)[:, None]
    col_index = jnp.arange(tile_width, dtype=jnp.int32)[None, :]
    lag_table = tile_width + row_index - col_index
    return windows[:, :, :, lag_table]


def convolve(rows_green, slips):
    count_rows = rows_green.shape[1]
    length = rows_green.shape[2]
    variations = slips.shape[0]
    tile_width = 128
    blocks = length // tile_width
    toeplitz_all = lag_tiles(rows_green, tile_width)
    pieces = slips.reshape(variations, count_rows, blocks, tile_width)
    result = jnp.zeros((variations, 2, blocks, tile_width), jnp.float32)
    for offset in range(blocks):
        partial_term = jnp.einsum(
            "hmij,vmaj->vhai",
            toeplitz_all[offset],
            pieces[:, :, : blocks - offset, :],
            preferred_element_type=jnp.float32,
        )
        result = result + jnp.pad(partial_term, ((0, 0), (0, 0), (offset, 0), (0, 0)))
    return result.reshape(variations, 2, length)


def on_device(green_tensor, moment, slip_rate, owner_shard, point_slot, live_counts):
    held_rows = slip_rate.shape[1]
    length = slip_rate.shape[2]
    variations = slip_rate.shape[0]
    shards = lax.axis_size("pt")
    capacity = 2 * held_rows // shards
    slots_total = shards * capacity
    live_rows = jnp.arange(held_rows, dtype=jnp.int32) < live_counts[0]
    slip_live = jnp.where(live_rows[None, :, None], slip_rate, jnp.zeros((), slip_rate.dtype))
    gathered_tensor, gathered_moment = (
        lax.all_gather(green_tensor, "var", axis=2, tiled=True),
        lax.all_gather(moment, "var", axis=1, tiled=True),
    )
    green_field = combine(gathered_tensor, gathered_moment)
    owners = owner_shard[:, 0]
    owner_table = (owners[:, None] == jnp.arange(shards, dtype=jnp.int32)[None, :]).astype(
        jnp.int32
    )
    position = jnp.sum(jnp.cumsum(owner_table, axis=0) * owner_table, axis=1) - 1
    buffer_index = owners * capacity + position
    slot_buffer = jnp.zeros((slots_total,), jnp.int32).at[buffer_index].set(point_slot)
    source_row = (
        jnp.full((slots_total,), held_rows, jnp.int32)
        .at[buffer_index]
        .set(jnp.arange(held_rows, dtype=jnp.int32))
    )
    outgoing = jnp.take(slip_live, source_row, axis=1, mode="fill", fill_value=0)
    outgoing = outgoing.reshape(variations, shards, capacity, length)
    arrived = lax.all_to_all(outgoing, "pt", split_axis=1, concat_axis=1, tiled=True)
    arrived_slots = lax.all_to_all(
        slot_buffer.reshape(1, shards, capacity), "pt", split_axis=1, concat_axis=1, tiled=True
    )
    rows_green = jnp.take(green_field, arrived_slots.reshape(-1), axis=1)
    partial_sums = convolve(rows_green, arrived.reshape(variations, slots_total, length))
    return lax.psum_scatter(partial_sums, "pt", scatter_dimension=2, tiled=True)


def solution(mesh):
    in_specs = (
        P(None, None, ("pt", "var"), None),
        P(None, ("pt", "var")),
        P("var", "pt", None),
        P("pt", None),
        P("pt"),
        P("pt"),
    )
    out_specs = P("var", None, "pt")
    return jax.shard_map(
        on_device, mesh=mesh, in_specs=in_specs, out_specs=out_specs, check_vma=False
    )
```

profile of v0, /device:TPU:1, one launch (start us, length us, event | category | flops | bytes accessed | tf_op | source)
XLA Modules:
  0.0 402.9 jit_solution(16042159017105554752)
XLA Ops:
  6.5 0.7 fusion.57
  7.3 0.1 reduce_window_sum.11
  7.3 0.8 select_reduce_fusion
  8.2 0.7 fusion.58
  8.8 0.8 scatter_custom_fusion.1
  9.6 0.7 reshape.120
  10.3 8.6 %all-to-all-start.1 = ((s32[1,32,2]{2,0,1:T(1,128)}), s32[1,32,2]{2,0,1:T(1,128)S(1)}, u32[]{:S(2)}, u32[]{:S(2)}) async-start(s32[1,32,2]{2,0,1:T(1,128)} %bitcast.7), calls=%async_computation.1 | async-start | bytes 32768 | tf_op jit(solution)/shard_map/all_to_all | solution.py:76
  18.9 0.7 scatter_custom_fusion
  20.3 0.1 broadcast_in_dim.51
  20.4 1.9 copy_select_fusion
  22.3 0.7 gather_fusion
  23.0 3.8 broadcast_select_fusion
  26.8 0.0 all-to-all-done.1
  26.8 7.5 %all-to-all-start = ((bf16[16,32,2,1024]{3,2,0,1:T(2,128)(2,1)}), bf16[16,32,2,1024]{3,2,0,1:T(2,128)(2,1)S(1)}, u32[]{:S(2)}, u32[]{:S(2)}) async-start(bf16[16,32,2,1024]{3,2,0,1:T(2,128)(2,1)} %broadcast_select_fusion), calls=%async_computation | async-start | bytes 4194304 | tf_op jit(solution)/shard_map/all_to_all | solution.py:75
  34.3 0.0 reduce-scatter.4.cloned.1.call-start
  34.3 13.5 %all_gather.7 = bf16[6,2,32,1024]{3,2,1,0:T(8,128)(2,1)S(1)} all-gather(bf16[6,2,8,1024]{3,2,1,0:T(8,128)(2,1)S(1)} %copy-done.5), channel_id=1, replica_groups=mesh['pt'=32,'var'=4] {'var'}, dimensions={2}, use_global_device_ids=true | all-gather | bytes 983040 | tf_op jit(solution)/shard_map/all_gather | solution.py:57
  47.9 0.1 copy.70
  48.0 9.0 %all_gather.6 = bf16[6,32]{0,1:T(8,128)(2,1)S(1)} all-gather(bf16[6,8]{0,1:T(8,128)(2,1)S(1)} %copy.70), channel_id=1, replica_groups=mesh['pt'=32,'var'=4] {'var'}, dimensions={1}, use_global_device_ids=true | all-gather | bytes 480 | tf_op jit(solution)/shard_map/all_gather | solution.py:58
  57.0 0.1 copy.71
  57.1 0.3 multiply_reduce_fusion
  57.3 0.1 copy.158
  57.5 0.1 fusion.56
  57.6 0.1 reshape.122
  57.7 0.5 broadcast.148
  58.2 0.7 reduce.5
  58.9 0.1 reshape.121
  59.0 1.1 gather_fusion.1
  60.1 0.3 fusion.54
  60.5 0.2 pad.32
  60.7 0.2 reshape.194
  60.9 0.1 fusion.64
  61.0 1.2 copy.125
  62.2 1.2 copy.126
  63.4 1.4 maximum_bitcast_fusion
  64.8 129.3 %gather_fusion.2 = bf16[16384,8,2,64]{3,1,2,0:T(8,128)(2,1)} fusion(bf16[8,2,64,256]{2,0,3,1:T(8,128)(2,1)S(1)} %maximum_bitcast_fusion, s32[16384]{0:T(1024)S(1)} %fusion.56), kind=kCustom, calls=%fused_computation.2 | custom fusion | bytes 67174400 | tf_op jit(solution)/shard_map/gather | solution.py:24
  194.1 59.5 %copy.106 = bf16[128,128,8,2,64]{1,0,4,3,2:T(8,128)(2,1)} copy(bf16[128,128,8,2,64]{4,2,3,1,0:T(8,128)(2,1)} %bitcast.12) | data formatting | bytes 67108864 | tf_op jit(solution)/shard_map/gather | solution.py:24
  253.6 0.0 all-to-all-done
  253.6 3.4 copy.68
  257.0 3.2 reshape_reshape.3
  260.2 1.5 slice_bitcast_fusion.18
  261.7 1.5 slice_bitcast_fusion.17
  263.1 1.4 slice_bitcast_fusion.16
  264.6 1.5 slice_bitcast_fusion.50
  266.1 0.4 slice_bitcast_fusion.49
  266.5 1.2 slice_bitcast_fusion.51
  267.7 1.2 slice.89
  269.0 3.4 reshape.168
  272.3 4.7 %fusion.36 = f32[16,7,2,128]{3,0,2,1:T(8,128)S(1)} fusion(bf16[8,2,64,128,128]{4,3,2,1,0:T(8,128)(2,1)} %bitcast.188, bf16[16,64,7,128,1]{3,2,1,0,4:T(8,128)(2,1)} %slice_bitcast_fusion.18), kind=kOutput, calls=%fused_computation.38 | convolution fusion | flops 469762048 | bytes 6406144 | tf_op jit(solution)/shard_map/hmij,vmaj->vhai/dot_general | solution.py:37
  277.0 0.1 copy.161
  277.1 4.0 fusion.39
  281.1 0.1 copy.160
  281.2 3.7 fusion.42
  284.9 0.1 copy.159
  285.0 3.7 fusion.45
  288.7 3.6 fusion.46
  292.4 3.6 fusion.47
  296.1 3.4 fusion.48
  299.5 3.7 fusion.33
  303.3 4.5 %copy.124 = f32[16,2,8,128]{1,0,3,2:T(8,128)} copy(f32[16,2,8,128]{3,2,1,0:T(8,128)S(1)} %fusion.33) | data formatting | bytes 262144
  307.8 7.1 %reshape.192 = f32[1024,32]{1,0:T(8,128)} reshape(f32[1024,16,2]{2,1,0:T(8,128)} %bitcast.196) | data formatting | bytes 262144
  314.8 0.0 reduce-scatter.4.cloned.1.call-update
  314.9 79.5 %reduce-scatter.4.cloned.1.call-done = f32[32,32]{1,0:T(8,128)} async-done(((f32[1024,32]{1,0:T(8,128)}), f32[32,32]{1,0:T(8,128)}) %reduce-scatter.4.cloned.1.call-update) | async-done | bytes 4112
  394.4 0.9 reshape.193
  395.2 0.8 copy.121
  (28 shorter events, 0.2 us)
Async XLA Ops:
  10.3 16.4 %all-to-all-start.1 = ((s32[1,32,2]{2,0,1:T(1,128)}), s32[1,32,2]{2,0,1:T(1,128)S(1)}, u32[]{:S(2)}, u32[]{:S(2)}) async-start(s32[1,32,2]{2,0,1:T(1,128)} %bitcast.7), calls=%async_computation.1 | async-start | bytes 32768 | tf_op jit(solution)/shard_map/all_to_all | solution.py:76
  26.8 7.6 %copy-start.5 = (bf16[6,2,8,1024]{3,2,1,0:T(8,128)(2,1)S(1)}, bf16[6,2,8,1024]{3,2,1,0:T(8,128)(2,1)}, u32[]{:S(2)}) copy-start(bf16[6,2,8,1024]{3,2,1,0:T(8,128)(2,1)} %param.6) | copy-start | bytes 589828
  26.8 21.1 %copy-start.6 = (bf16[6,8]{1,0:T(8,128)(2,1)S(1)}, bf16[6,8]{1,0:T(8,128)(2,1)}, u32[]{:S(2)}) copy-start(bf16[6,8]{1,0:T(8,128)(2,1)} %param.7) | copy-start | bytes 292
  26.8 226.9 %all-to-all-start = ((bf16[16,32,2,1024]{3,2,0,1:T(2,128)(2,1)}), bf16[16,32,2,1024]{3,2,0,1:T(2,128)(2,1)S(1)}, u32[]{:S(2)}, u32[]{:S(2)}) async-start(bf16[16,32,2,1024]{3,2,0,1:T(2,128)(2,1)} %broadcast_select_fusion), calls=%async_computation | async-start | bytes 4194304 | tf_op jit(solution)/shard_map/all_to_all | solution.py:75
  34.3 360.1 %reduce-scatter.4.cloned.1.call-start = ((), (), s32[]{:S(2)}) async-start(), calls=%async_computation.3 | async-start | bytes 540672
  272.3 4.8 %copy-start.1 = (bf16[16,64,6,128,1]{3,2,1,0,4:T(8,128)(2,1)S(1)}, bf16[16,64,6,128,1]{3,2,1,0,4:T(8,128)(2,1)}, u32[]{:S(2)}) copy-start(bf16[16,64,6,128,1]{3,2,1,0,4:T(8,128)(2,1)} %slice_bitcast_fusion.17) | copy-start | bytes 4718596
  277.1 4.1 %copy-start = (bf16[16,64,5,128,1]{3,2,1,0,4:T(8,128)(2,1)S(1)}, bf16[16,64,5,128,1]{3,2,1,0,4:T(8,128)(2,1)}, u32[]{:S(2)}) copy-start(bf16[16,64,5,128,1]{3,2,1,0,4:T(8,128)(2,1)} %slice_bitcast_fusion.16) | copy-start | bytes 3932164
  281.2 3.8 copy-start.2
  288.7 3.7 copy-start.4
  292.4 3.7 copy-start.3
Sparse Core Ops, SparseCore 0:
  315.0 79.3 reduce-scatter.3
where the time goes:
time: 406 us; the launch traced here: 403 us
  local copies, waits for them, and re-layouts  229 us (56%)
  waiting for transfers between devices  79.5 us (20%)
  matrix products  30.4 us (7%)
  blocking collectives  22.5 us (6%)
  starting transfers between devices  16.1 us (4%)
  between operations  14.4 us (4%)
  other arithmetic  10.7 us (3%)
    gather x2, local copies, waits for them, and re-layouts, lag_tiles(): return windows[:, :, :, lag_table]  189 us
    unnamed x2, waiting for transfers between devices  79.5 us
    dot_general x8, matrix products, convolve(): jnp.einsum('hmij,vmaj->vhai', toeplitz_all[offset], pieces[:, :, :blocks...  30.4 us
    unnamed x21, local copies, waits for them, and re-layouts  15.7 us
    all_gather x1, blocking collectives, on_device(): lax.all_gather(green_tensor, 'var', axis=2, tiled=True)  13.5 us
    all_gather x1, blocking collectives, on_device(): lax.all_gather(moment, 'var', axis=1, tiled=True)  8.97 us
    slice x7, local copies, waits for them, and re-layouts, convolve(): pieces[:, :, :blocks - offset, :]  8.77 us
    all_to_all x1, starting transfers between devices, on_device(): lax.all_to_all(slot_buffer.reshape(1, shards, capacity), 'pt', split_axis...  8.59 us
  transfers between devices with their start and end apart: 3, of which 1 were waited for; matrix products, arithmetic and copies ran while one was open for 51% of the time, Pallas kernels for 0%

commit v1 on v0

v1 whole, which is shorter than its diff:
```python
import functools

import jax
import jax.numpy as jnp
from jax import lax
from jax.experimental import pallas as pl
from jax.experimental.pallas import tpu as pltpu
from jax.sharding import PartitionSpec as P

F32 = jnp.float32
BF16 = jnp.bfloat16
LANES = 128
N_PT = 32
N_VAR = 4
HELD = 32
OWN = 8
BLOCKS = 8
VARS = 16
MESH = pl.DeviceIdType.MESH


def request_table(owner_ref, slot_ref):
    row = lax.broadcasted_iota(jnp.int32, (N_PT, LANES), 0)
    lane = lax.broadcasted_iota(jnp.int32, (N_PT, LANES), 1)
    table = jnp.zeros((N_PT, LANES), jnp.int32)
    count = jnp.zeros((N_PT, LANES), jnp.int32)
    for r in range(HELD):
        hit = row == owner_ref[r, 0]
        table = jnp.where(hit & (lane == count), slot_ref[r], table)
        count = count + hit.astype(jnp.int32)
    return table


def kernel(
    slip_hbm, green_hbm, moment_ref, owner_ref, slot_ref, live_ref, out_ref,
    slip, green, fold, field, ask, asked, asked_s, pick_s, outbox, inbox,
    gathered, xmat, gmat, zmat, part, landed,
    slip_sem, green_sem, ask_sem, z_send, z_recv, q_send, q_recv, g_send, g_recv, y_send, y_recv,
):
    me = lax.axis_index("pt")
    level = lax.axis_index("var")

    slip_copy = pltpu.make_async_copy(slip_hbm, slip, slip_sem)
    green_copy = pltpu.make_async_copy(green_hbm, green, green_sem)
    green_copy.start()
    slip_copy.start()

    barrier = pltpu.get_barrier_semaphore()

    def greet(k, carry):
        pl.semaphore_signal(barrier, inc=1, device_id={"pt": lax.rem(me + k, N_PT)}, device_id_type=MESH)
        return carry

    lax.fori_loop(1, N_PT, greet, 0)
    for d in range(1, N_VAR):
        pl.semaphore_signal(barrier, inc=1, device_id={"var": lax.rem(level + d, N_VAR)}, device_id_type=MESH)

    table = request_table(owner_ref, slot_ref)
    for o in range(N_PT):
        ask[o] = table[o : o + 1, :]
    seen = jnp.int32(0)
    for r in range(HELD):
        owner = owner_ref[r, 0]
        bit = jnp.left_shift(jnp.int32(1), owner)
        second = jnp.where((seen & bit) != 0, 1, 0)
        seen = seen | bit
        place = lax.rem(me + (2 * N_PT - 1) - owner, N_PT)
        pick_s[r] = jnp.where(r < live_ref[0], 2 * place + second, 2 * N_PT)

    green_copy.wait()
    tall = jnp.transpose(moment_ref[...].astype(F32))
    tall = jnp.concatenate([tall, tall], axis=0)
    for m in range(BLOCKS):
        total = jnp.zeros((2 * OWN, LANES), F32)
        for c in range(6):
            total = total + tall[:, c : c + 1] * green[16 * c : 16 * c + 16, LANES * m : LANES * (m + 1)].astype(F32)
        fold[16 * m : 16 * m + 16, :] = total
    for p in range(OWN):
        one = jnp.concatenate(
            [fold[pl.ds(p, BLOCKS, stride=16), :], fold[pl.ds(8 + p, BLOCKS, stride=16), :]], axis=0
        )
        field[level * OWN + p] = one.astype(BF16)

    pl.semaphore_wait(barrier, N_PT - 1 + N_VAR - 1)

    for d in range(1, N_VAR):
        pltpu.make_async_remote_copy(
            src_ref=field.at[pl.ds(level * OWN, OWN)],
            dst_ref=field.at[pl.ds(level * OWN, OWN)],
            send_sem=z_send.at[d - 1],
            recv_sem=z_recv.at[d - 1],
            device_id={"var": lax.rem(level + d, N_VAR)},
            device_id_type=MESH,
        ).start()

    def send_ask(k, carry):
        other = lax.rem(me + k, N_PT)
        pltpu.make_async_remote_copy(
            src_ref=ask.at[other],
            dst_ref=asked.at[k - 1],
            send_sem=q_send,
            recv_sem=q_recv,
            device_id={"pt": other},
            device_id_type=MESH,
        ).start()
        return carry

    lax.fori_loop(1, N_PT, send_ask, 0)
    asked[N_PT - 1] = ask[me]

    slip_copy.wait()
    lane16 = lax.broadcasted_iota(jnp.int32, (16, LANES), 1) // 32

    def turn(g, carry):
        for n in range(BLOCKS):
            piece = slip[pl.ds(4 * g, 4), :, LANES * n : LANES * (n + 1)].reshape(LANES, LANES)
            flipped = jnp.transpose(piece)
            for half in range(2):
                rows = [flipped[16 * (4 * half + q) : 16 * (4 * half + q) + 16, :] for q in range(4)]
                for v in range(4):
                    mixed = rows[v]
                    for q in range(4):
                        if q != v:
                            mixed = jnp.where(lane16 == q, pltpu.roll(rows[q], 32 * ((q - v) % 4), 1), mixed)
                    xmat[
                        pl.ds(pl.multiple_of((4 * g + v) * 16, 16), 16),
                        256 * (BLOCKS - 1 - n) + LANES * half : 256 * (BLOCKS - 1 - n) + LANES * (half + 1),
                    ] = mixed
        return carry

    lax.fori_loop(0, 4, turn, 0)

    everyone = pltpu.make_async_remote_copy(
        src_ref=ask.at[pl.ds(0, N_PT - 1)], dst_ref=asked.at[pl.ds(0, N_PT - 1)], send_sem=q_send, recv_sem=q_recv,
        device_id={"pt": lax.rem(me + 1, N_PT)}, device_id_type=MESH,
    )
    everyone.wait_recv()
    to_scalar = pltpu.make_async_copy(asked, asked_s, ask_sem)
    to_scalar.start()
    for d in range(1, N_VAR):
        source = lax.rem(level + (N_VAR - d), N_VAR)
        pltpu.make_async_remote_copy(
            src_ref=field.at[pl.ds(level * OWN, OWN)],
            dst_ref=field.at[pl.ds(source * OWN, OWN)],
            send_sem=z_send.at[d - 1],
            recv_sem=z_recv.at[d - 1],
            device_id={"var": lax.rem(level + d, N_VAR)},
            device_id_type=MESH,
        ).wait()
    to_scalar.wait()

    def serve(k, carry):
        other = lax.rem(me + k, N_PT)
        for s in range(2):
            outbox[2 * (k - 1) + s] = field[asked_s[N_PT - 1 - k, 0, s]]
        pltpu.make_async_remote_copy(
            src_ref=outbox.at[pl.ds(2 * (k - 1), 2)],
            dst_ref=inbox.at[pl.ds(2 * (k - 1), 2)],
            send_sem=g_send,
            recv_sem=g_recv,
            device_id={"pt": other},
            device_id_type=MESH,
        ).start()
        return carry

    lax.fori_loop(1, N_PT, serve, 0)
    for s in range(2):
        inbox[2 * (N_PT - 1) + s] = field[asked_s[N_PT - 1, 0, s]]
    inbox[2 * N_PT] = jnp.zeros((16, LANES), BF16)

    boxes = pltpu.make_async_remote_copy(
        src_ref=outbox.at[pl.ds(0, 2 * (N_PT - 1))], dst_ref=inbox.at[pl.ds(0, 2 * (N_PT - 1))],
        send_sem=g_send, recv_sem=g_recv, device_id={"pt": lax.rem(me + 1, N_PT)}, device_id_type=MESH,
    )
    boxes.wait_recv()
    everyone.wait_send()

    for r in range(HELD):
        gathered[16 * r : 16 * r + 16, :] = inbox[pick_s[r]].astype(F32)
    lane32 = lax.broadcasted_iota(jnp.int32, (HELD, LANES), 1)
    for h in range(2):
        before = None
        for m in range(BLOCKS):
            here = gathered[pl.ds(BLOCKS * h + m, HELD, stride=16), :].astype(BF16)
            for c in range(BLOCKS):
                if c == 0:
                    delayed = here
                else:
                    now = pltpu.roll(here, 16 * c, 1)
                    then = jnp.zeros_like(now) if before is None else pltpu.roll(before, 16 * c, 1)
                    delayed = jnp.where(lane32 >= 16 * c, now, then)
                gmat[256 * m + 32 * c : 256 * m + 32 * c + 32, LANES * h : LANES * (h + 1)] = delayed
            before = here

    wide = lax.broadcasted_iota(jnp.int32, (VARS, 2 * LANES), 1) % LANES
    group8 = lax.broadcasted_iota(jnp.int32, (8, LANES), 1) // 32
    spill = jnp.zeros((VARS, 2 * LANES), F32)
    for m in range(BLOCKS):
        product = jnp.dot(
            xmat[:, 256 * (BLOCKS - 1 - m) :], gmat[: 256 * (m + 1), :], preferred_element_type=F32
        )
        zmat[m % 2, 0] = product[:, :LANES]
        zmat[m % 2, 1] = product[:, LANES:]
        total = spill
        spill = jnp.zeros((VARS, 2 * LANES), F32)
        for f in range(16):
            rows = [zmat[m % 2, h, pl.ds(f, VARS, stride=16), :] for h in range(2)]
            if f == 0:
                total = total + jnp.concatenate(rows, axis=1)
            else:
                rolled = jnp.concatenate([pltpu.roll(rows[h], f, 1) for h in range(2)], axis=1)
                kept = jnp.where(wide >= f, rolled, 0.0)
                total = total + kept
                spill = spill + (rolled - kept)
        quarters = [total[8 * (q // 2) : 8 * (q // 2) + 8, LANES * (q % 2) : LANES * (q % 2) + LANES] for q in range(4)]
        for t in range(4):
            mixed = quarters[t]
            for q in range(4):
                if q != t:
                    mixed = jnp.where(group8 == q, pltpu.roll(quarters[q], 32 * ((q - t) % 4), 1), mixed)
            part[4 * m + t] = mixed

    def hand_out(k, carry):
        other = lax.rem(me + k, N_PT)
        pltpu.make_async_remote_copy(
            src_ref=part.at[other],
            dst_ref=landed.at[k - 1],
            send_sem=y_send,
            recv_sem=y_recv,
            device_id={"pt": other},
            device_id_type=MESH,
        ).start()
        return carry

    lax.fori_loop(1, N_PT, hand_out, 0)
    mine = part[me]
    boxes.wait_send()
    parts = pltpu.make_async_remote_copy(
        src_ref=part.at[pl.ds(0, N_PT - 1)], dst_ref=landed.at[pl.ds(0, N_PT - 1)],
        send_sem=y_send, recv_sem=y_recv, device_id={"pt": lax.rem(me + 1, N_PT)}, device_id_type=MESH,
    )
    parts.wait_recv()
    out_ref[...] = mine + jnp.sum(landed[...], axis=0)
    parts.wait_send()


def on_device(green_tensor, moment, slip_rate, owner_shard, point_slot, live_counts):
    hbm = pl.BlockSpec(memory_space=pl.ANY)
    vmem = pl.BlockSpec(memory_space=pltpu.VMEM)
    smem = pl.BlockSpec(memory_space=pltpu.SMEM)
    dma = pltpu.SemaphoreType.DMA
    length = slip_rate.shape[2]
    packed = pl.pallas_call(
        kernel,
        out_shape=jax.ShapeDtypeStruct((8, LANES), F32),
        in_specs=[hbm, hbm, vmem, smem, smem, smem],
        out_specs=vmem,
        scratch_shapes=[
            pltpu.VMEM((VARS, HELD, length), BF16),
            pltpu.VMEM((96, length), BF16),
            pltpu.VMEM((LANES, LANES), F32),
            pltpu.VMEM((HELD, 16, LANES), BF16),
            pltpu.VMEM((N_PT, 1, LANES), jnp.int32),
            pltpu.VMEM((N_PT, 1, LANES), jnp.int32),
            pltpu.SMEM((N_PT, 1, LANES), jnp.int32),
            pltpu.SMEM((HELD,), jnp.int32),
            pltpu.VMEM((2 * (N_PT - 1), 16, LANES), BF16),
            pltpu.VMEM((2 * N_PT + 1, 16, LANES), BF16),
            pltpu.VMEM((HELD * 16, LANES), F32),
            pltpu.VMEM((VARS * 16, 256 * BLOCKS), BF16),
            pltpu.VMEM((256 * BLOCKS, 2 * LANES), BF16),
            pltpu.VMEM((2, 2, VARS * 16, LANES), F32),
            pltpu.VMEM((N_PT, 8, LANES), F32),
            pltpu.VMEM((N_PT - 1, 8, LANES), F32),
            dma, dma, dma, dma((N_VAR - 1,)), dma((N_VAR - 1,)), dma, dma, dma, dma, dma, dma,
        ],
        compiler_params=pltpu.CompilerParams(
            collective_id=0, has_side_effects=True, vmem_limit_bytes=32 * 1024 * 1024
        ),
        name="synthesis",
    )(slip_rate, green_tensor.reshape(96, length), moment, owner_shard, point_slot, live_counts)
    return packed.reshape(8, 2, 2, 32).transpose(1, 0, 2, 3).reshape(VARS, 2, 32)


def solution(mesh):
    in_specs = (
        P(None, None, ("pt", "var"), None),
        P(None, ("pt", "var")),
        P("var", "pt", None),
        P("pt", None),
        P("pt"),
        P("pt"),
    )
    out_specs = P("var", None, "pt")
    return jax.shard_map(on_device, mesh=mesh, in_specs=in_specs, out_specs=out_specs, check_vma=False)
```

time: 406 us -> 33.4 us (0.08)
  local copies, waits for them, and re-layouts: 229 us -> 4.17 us
  waiting for transfers between devices: 79.5 us -> 0 us
  matrix products: 30.4 us -> 0 us
  Pallas kernels: 0 us -> 28.3 us
  blocking collectives: 22.5 us -> 0 us
  starting transfers between devices: 16.1 us -> 0 us
  between operations: 14.4 us -> 0.68 us
  other arithmetic: 10.7 us -> 0 us
    gather x4 -> x0, local copies, waits for them, and re-layouts: 191 us -> none  [the longest x2 189 us: lag_tiles(): return windows[:, :, :, lag_table]]
    unnamed x2 -> x0, waiting for transfers between devices: 79.5 us -> none
    dot_general x8 -> x0, matrix products: 30.4 us -> none  [convolve(): jnp.einsum('hmij,vmaj->vhai', toeplitz_all[offset], pieces[:, :, :blocks...]
    pallas_call x0 -> x1, Pallas kernels: none -> 28.3 us  [on_device(): pl.pallas_call(kernel, out_shape=jax.ShapeDtypeStruct((8, LANES), F32), i...]
    all_gather x2 -> x0, blocking collectives: 22.5 us -> none  [the longest x1 13.5 us: on_device(): lax.all_gather(green_tensor, 'var', axis=2, tiled=True)]
    all_to_all x2 -> x0, starting transfers between devices: 16.1 us -> none  [the longest x1 8.59 us: on_device(): lax.all_to_all(slot_buffer.reshape(1, shards, capacity), 'pt', split_axis...]
    unnamed x21 -> x11, local copies, waits for them, and re-layouts: 15.7 us -> 3.48 us
    slice x8 -> x0, local copies, waits for them, and re-layouts: 8.88 us -> none  [the longest x7 8.77 us: convolve(): pieces[:, :, :blocks - offset, :]]
  transfers between devices with their start and end apart: 3 -> 0, of which waited for: 1 -> 0; matrix products, arithmetic and copies ran while one was open for 51% -> 0% of each run, Pallas kernels for 0% -> 0%
where the time goes in v1:
time: 33.4 us; the launch traced here: 33.2 us
  Pallas kernels  28.3 us (85%)
  local copies, waits for them, and re-layouts  4.17 us (12%)
  between operations  0.68 us (2%)
    pallas_call x1, Pallas kernels, on_device(): pl.pallas_call(kernel, out_shape=jax.ShapeDtypeStruct((8, LANES), F32), i...  28.3 us
    unnamed x11, local copies, waits for them, and re-layouts  3.48 us

profile of v1, /device:TPU:1, one launch (start us, length us, event | category | flops | bytes accessed | tf_op | source)
XLA Modules:
  0.0 33.2 jit_solution(13318476456890108568)
XLA Ops:
  0.7 0.0 copy-start.4
  0.7 0.6 %copy-done.4 = s32[32,1]{0,1:T(1,128)S(1)} copy-done((s32[32,1]{0,1:T(1,128)S(1)}, s32[32,1]{0,1:T(1,128)}, u32[]{:S(2)}) %copy-start.4) | copy-done | bytes 152
  1.3 0.0 copy-start.2
  1.3 0.0 copy-start.3
  1.3 0.1 copy.7.owner_ref
  1.4 0.6 %copy-done.2 = bf16[6,8]{1,0:T(8,128)(2,1)S(1)} copy-done((bf16[6,8]{1,0:T(8,128)(2,1)S(1)}, bf16[6,8]{1,0:T(8,128)(2,1)}, u32[]{:S(2)}) %copy-start.2) | copy-done | bytes 120
  2.0 0.0 copy-done.3
  2.0 0.0 copy-start
  2.0 1.2 %copy-done = bf16[16,32,1024]{2,1,0:T(8,128)(2,1)S(1)} copy-done((bf16[16,32,1024]{2,1,0:T(8,128)(2,1)S(1)}, bf16[16,32,1024]{2,1,0:T(8,128)(2,1)}, u32[]{:S(2)}) %copy-start) | copy-done | bytes 1048600
  3.2 0.0 copy-start.1
  3.2 0.9 %copy-done.1 = bf16[6,2,8,1024]{3,2,1,0:T(8,128)(2,1)S(1)} copy-done((bf16[6,2,8,1024]{3,2,1,0:T(8,128)(2,1)S(1)}, bf16[6,2,8,1024]{3,2,1,0:T(8,128)(2,1)}, u32[]{:S(2)}) %copy-start.1) | copy-done | bytes 196632
  4.1 28.3 %synthesis.1 = f32[8,128]{1,0:T(8,128)S(1)} custom-call(bf16[16,32,1024]{2,1,0:T(8,128)(2,1)S(1)} %copy-done, bf16[96,1024]{1,0:T(8,128)(2,1)S(1)} %bitcast.3, bf16[6,8]{1,0:T(8,128)(2,1)S(1)} %copy-done.2, s32[32,1]{1,0:T(8,128)S(1)} %copy.7.owner_ref, s32[32]{0:T(128)S(1)} %copy-done.3, s32[1]{0:T(128)S(6)} %copy.9.live_ref), custom_call_target="tpu_custom_call" | custom-call | tf_op jit(solution)/shard_map/synthesis/pallas_call | solution.py:253
  32.5 0.1 reshape.10
  32.5 0.6 %copy.8 = f32[2,8,2,32]{3,2,1,0:T(2,128)} copy(f32[2,8,2,32]{3,2,0,1:T(2,128)S(1)} %bitcast.4) | data formatting | bytes 8192 | tf_op jit(solution)/shard_map/transpose | solution.py:282
Async XLA Ops:
  0.7 0.7 %copy-start.4 = (s32[32,1]{0,1:T(1,128)S(1)}, s32[32,1]{0,1:T(1,128)}, u32[]{:S(2)}) copy-start(s32[32,1]{0,1:T(1,128)} %param.9) | copy-start | bytes 388
  1.3 0.7 %copy-start.2 = (bf16[6,8]{1,0:T(8,128)(2,1)S(1)}, bf16[6,8]{1,0:T(8,128)(2,1)}, u32[]{:S(2)}) copy-start(bf16[6,8]{1,0:T(8,128)(2,1)} %moment_ref.1) | copy-start | bytes 292
  1.3 0.7 %copy-start.3 = (s32[32]{0:T(128)S(1)}, s32[32]{0:T(128)}, u32[]{:S(2)}) copy-start(s32[32]{0:T(128)} %slot_ref.1) | copy-start | bytes 388
  2.0 1.2 %copy-start = (bf16[16,32,1024]{2,1,0:T(8,128)(2,1)S(1)}, bf16[16,32,1024]{2,1,0:T(8,128)(2,1)}, u32[]{:S(2)}) copy-start(bf16[16,32,1024]{2,1,0:T(8,128)(2,1)} %slip_hbm.1) | copy-start | bytes 3145732
  3.2 0.9 %copy-start.1 = (bf16[6,2,8,1024]{3,2,1,0:T(8,128)(2,1)S(1)}, bf16[6,2,8,1024]{3,2,1,0:T(8,128)(2,1)}, u32[]{:S(2)}) copy-start(bf16[6,2,8,1024]{3,2,1,0:T(8,128)(2,1)} %param.6) | copy-start | bytes 589828

commit v2 on v1

v2 whole, which is shorter than its diff:
```python
import functools

import jax
import jax.numpy as jnp
from jax import lax
from jax.experimental import pallas as pl
from jax.experimental.pallas import tpu as pltpu
from jax.sharding import PartitionSpec as P

F32 = jnp.float32
BF16 = jnp.bfloat16
LANES = 128
N_PT = 32
N_VAR = 4
HELD = 32
OWN = 8
BLOCKS = 8
VARS = 16
MESH = pl.DeviceIdType.MESH


def each_offset(body):
    def odd(q):
        return 1 + 2 * lax.rem(q, 2)

    def run(count, pair):
        def step(i, carry):
            dx, dy = pair(lax.div(i, 2))
            body(dx, dy, lax.rem(i, 2))
            return carry

        lax.fori_loop(0, count, step, 0)

    run(2, lambda q: (2, 2))
    run(8, lambda q: (2 + lax.div(q, 2) * (odd(q) - 2), odd(q) + lax.div(q, 2) * (2 - odd(q))))
    run(8, lambda q: (1 + 2 * lax.div(q, 2), odd(q)))
    run(4, lambda q: (2 * lax.rem(q, 2), 2 - 2 * lax.rem(q, 2)))
    run(8, lambda q: (lax.div(q, 2) * odd(q), (1 - lax.div(q, 2)) * odd(q)))
    body(0, 0, 1)


def code(dx, dy, dc):
    return lax.rem(8 * dx + 2 * dy + dc + N_PT - 1, N_PT)


def request_table(owner_ref, slot_ref):
    row = lax.broadcasted_iota(jnp.int32, (N_PT, LANES), 0)
    lane = lax.broadcasted_iota(jnp.int32, (N_PT, LANES), 1)
    table = jnp.zeros((N_PT, LANES), jnp.int32)
    count = jnp.zeros((N_PT, LANES), jnp.int32)
    for r in range(HELD):
        hit = row == owner_ref[0, r]
        table = jnp.where(hit & (lane == count), slot_ref[r], table)
        count = count + hit.astype(jnp.int32)
    return table


def kernel(
    slip_hbm, green_hbm, moment_hbm, owner_hbm, slot_hbm, live_ref, out_ref,
    slip, green, moment, owner_ref, slot_ref, fold, field, ask, asked_v, asked, pick_s, second_s, field32, outbox, inbox_0, inbox_1,
    gathered, xmat, gmat, zmat, part, landed,
    slip_sem, green_sem, small_sem, ask_sem, z_send, z_recv, q_send, q_recv, g_send, g_recv, y_send, y_recv,
):
    me = lax.axis_index("pt")
    level = lax.axis_index("var")
    at_x, at_y, at_c = lax.div(me, 8), lax.rem(lax.div(me, 2), 4), lax.rem(me, 2)

    def peer(dx, dy, dc):
        return 8 * lax.rem(at_x + dx, 4) + 2 * lax.rem(at_y + dy, 4) + lax.rem(at_c + dc, 2)

    def above(d):
        return {"var": lax.rem(level + d, N_VAR)}

    sibling = {"pt": peer(0, 0, 1)}

    slip_copy = pltpu.make_async_copy(slip_hbm, slip, slip_sem)
    green_copy = pltpu.make_async_copy(green_hbm, green, green_sem)
    small = [
        pltpu.make_async_copy(source, here, small_sem.at[i])
        for i, (source, here) in enumerate(
            [(owner_hbm, owner_ref), (slot_hbm, slot_ref), (moment_hbm, moment)]
        )
    ]
    for one in small:
        one.start()
    green_copy.start()
    slip_copy.start()

    barrier = pltpu.get_barrier_semaphore()

    def greet(dx, dy, dc):
        pl.semaphore_signal(barrier, inc=1, device_id={"pt": peer(dx, dy, dc)}, device_id_type=MESH)

    each_offset(greet)
    for d in range(1, N_VAR):
        pl.semaphore_signal(barrier, inc=1, device_id=above(d), device_id_type=MESH)

    for one in small:
        one.wait()
    table = request_table(owner_ref, slot_ref)
    for o in range(N_PT):
        ask[o] = table[o : o + 1, :]
    seen = jnp.int32(0)
    for r in range(HELD):
        owner = owner_ref[0, r]
        bit = jnp.left_shift(jnp.int32(1), owner)
        second = jnp.where((seen & bit) != 0, 1, 0)
        seen = seen | bit
        place = (
            8 * lax.rem(at_x + 4 - lax.div(owner, 8), 4)
            + 2 * lax.rem(at_y + 4 - lax.rem(lax.div(owner, 2), 4), 4)
            + lax.rem(at_c + lax.rem(owner, 2), 2)
        )
        place = lax.rem(place + N_PT - 1, N_PT)
        pick_s[r] = jnp.where(r < live_ref[0], place, N_PT)
        second_s[r] = second

    green_copy.wait()
    tall = jnp.transpose(moment[...].astype(F32))
    tall = jnp.concatenate([tall, tall], axis=0)
    for m in range(BLOCKS):
        total = jnp.zeros((2 * OWN, LANES), F32)
        for c in range(6):
            total = total + tall[:, c : c + 1] * green[16 * c : 16 * c + 16, LANES * m : LANES * (m + 1)].astype(F32)
        for h in range(2):
            row = OWN * (8 * (m // 4) + 4 * h + m % 4)
            fold[row : row + OWN, :] = total[OWN * h : OWN * h + OWN]
    for p in range(OWN):
        one = jnp.concatenate([fold[pl.ds(p, 8, stride=OWN), :], fold[pl.ds(64 + p, 8, stride=OWN), :]], axis=0)
        field[level * OWN + p] = one.astype(BF16)

    pl.semaphore_wait(barrier, N_PT - 1 + N_VAR - 1)

    def send_ask(dx, dy, dc):
        other = peer(dx, dy, dc)
        pltpu.make_async_remote_copy(
            src_ref=ask.at[other], dst_ref=asked_v.at[code(dx, dy, dc)], send_sem=q_send, recv_sem=q_recv,
            device_id={"pt": other}, device_id_type=MESH,
        ).start()

    each_offset(send_ask)
    asked_v[N_PT - 1] = ask[me]
    spread = [
        pltpu.make_async_remote_copy(
            src_ref=field.at[pl.ds(level * OWN, OWN)], dst_ref=field.at[pl.ds(level * OWN, OWN)],
            send_sem=z_send.at[d - 1], recv_sem=z_recv.at[d - 1], device_id=above(d), device_id_type=MESH,
        )
        for d in range(1, N_VAR)
    ]
    for copy in spread:
        copy.start()

    slip_copy.wait()
    lane16 = lax.broadcasted_iota(jnp.int32, (16, LANES), 1) // 32

    def turn(g, carry):
        for n in range(BLOCKS):
            piece = slip[pl.ds(4 * g, 4), :, LANES * n : LANES * (n + 1)].reshape(LANES, LANES)
            flipped = jnp.transpose(piece)
            for half in range(2):
                rows = [flipped[16 * (4 * half + q) : 16 * (4 * half + q) + 16, :] for q in range(4)]
                for v in range(4):
                    mixed = rows[v]
                    for q in range(4):
                        if q != v:
                            mixed = jnp.where(lane16 == q, pltpu.roll(rows[q], 32 * ((q - v) % 4), 1), mixed)
                    xmat[
                        pl.ds(pl.multiple_of((4 * g + v) * 16, 16), 16),
                        256 * (BLOCKS - 1 - n) + LANES * half : 256 * (BLOCKS - 1 - n) + LANES * (half + 1),
                    ] = mixed
        return carry

    lax.fori_loop(0, 4, turn, 0)

    everyone = pltpu.make_async_remote_copy(
        src_ref=ask.at[pl.ds(0, N_PT - 1)], dst_ref=asked_v.at[pl.ds(0, N_PT - 1)], send_sem=q_send, recv_sem=q_recv,
        device_id=sibling, device_id_type=MESH,
    )
    everyone.wait_recv()
    to_scalar = pltpu.make_async_copy(asked_v, asked, ask_sem)
    to_scalar.start()
    for d in range(1, N_VAR):
        source = lax.rem(level + (N_VAR - d), N_VAR)
        pltpu.make_async_remote_copy(
            src_ref=field.at[pl.ds(level * OWN, OWN)], dst_ref=field.at[pl.ds(source * OWN, OWN)],
            send_sem=z_send.at[d - 1], recv_sem=z_recv.at[d - 1], device_id=above(d), device_id_type=MESH,
        ).wait_recv()

    for p in range(HELD):
        field32[p] = field[p].astype(F32)
    to_scalar.wait()

    def answer(where, half):
        rows = [field32[asked[where, 0, slot], 8 * half : 8 * half + 8, :] for slot in range(2)]
        return jnp.concatenate(rows, axis=0).astype(BF16)

    inbox = [inbox_0, inbox_1]
    for half in range(2):

        def serve(dx, dy, dc):
            place = code(dx, dy, dc)
            outbox[half, place] = answer(code(lax.rem(4 - dx, 4), lax.rem(4 - dy, 4), dc), half)
            pltpu.make_async_remote_copy(
                src_ref=outbox.at[half, place], dst_ref=inbox[half].at[place],
                send_sem=g_send.at[half], recv_sem=g_recv.at[half], device_id={"pt": peer(dx, dy, dc)},
                device_id_type=MESH,
            ).start()

        each_offset(serve)
    for half in range(2):
        inbox[half][N_PT - 1] = answer(N_PT - 1, half)
        inbox[half][N_PT] = jnp.zeros((16, LANES), BF16)
    boxes = [
        pltpu.make_async_remote_copy(
            src_ref=outbox.at[half], dst_ref=inbox[half].at[pl.ds(0, N_PT - 1)],
            send_sem=g_send.at[half], recv_sem=g_recv.at[half], device_id=sibling, device_id_type=MESH,
        )
        for half in range(2)
    ]
    everyone.wait_send()
    for copy in spread:
        copy.wait_send()

    lane32 = lax.broadcasted_iota(jnp.int32, (HELD, LANES), 1)
    wide = lax.broadcasted_iota(jnp.int32, (VARS, 2 * LANES), 1) % LANES
    group8 = lax.broadcasted_iota(jnp.int32, (8, LANES), 1) // 32

    def delay(half, before):
        for r in range(HELD):
            both = inbox[half][pick_s[r]].astype(F32)
            gathered[8 * r : 8 * r + 8, :] = jnp.where(second_s[r] == 1, both[8:], both[:8])
        last = []
        for h in range(2):
            previous = before[h]
            for m in range(4 * half, 4 * half + 4):
                here = gathered[pl.ds(4 * h + m % 4, HELD, stride=8), :].astype(BF16)
                for c in range(BLOCKS):
                    if c == 0:
                        delayed = here
                    else:
                        delayed = jnp.where(
                            lane32 >= 16 * c, pltpu.roll(here, 16 * c, 1), pltpu.roll(previous, 16 * c, 1)
                        )
                    gmat[256 * m + 32 * c : 256 * m + 32 * c + 32, LANES * h : LANES * (h + 1)] = delayed
                previous = here
            last.append(previous)
        return last

    def product(m, first, last):
        start = 256 * (BLOCKS - 1 - m + first)
        return jnp.dot(
            xmat[:, start : start + 256 * (last - first)], gmat[256 * first : 256 * last, :], preferred_element_type=F32
        )

    def finish(m, spill):
        total = spill
        spill = jnp.zeros((VARS, 2 * LANES), F32)
        for f in range(16):
            rows = [zmat[m, h, pl.ds(f, VARS, stride=16), :] for h in range(2)]
            if f == 0:
                total = total + jnp.concatenate(rows, axis=1)
            else:
                rolled = jnp.concatenate([pltpu.roll(rows[h], f, 1) for h in range(2)], axis=1)
                kept = jnp.where(wide >= f, rolled, 0.0)
                total = total + kept
                spill = spill + (rolled - kept)
        quarters = [total[8 * (q // 2) : 8 * (q // 2) + 8, LANES * (q % 2) : LANES * (q % 2) + LANES] for q in range(4)]
        for t in range(4):
            mixed = quarters[t]
            for q in range(4):
                if q != t:
                    mixed = jnp.where(group8 == q, pltpu.roll(quarters[q], 32 * ((q - t) % 4), 1), mixed)
            part[4 * m + t] = mixed
        return spill

    def hand_out(half):
        def step(i, carry):
            other = (N_PT // 2) * half + lax.rem(me + i, N_PT // 2)
            place = (
                8 * lax.rem(lax.div(other, 8) + 4 - at_x, 4)
                + 2 * lax.rem(lax.rem(lax.div(other, 2), 4) + 4 - at_y, 4)
                + lax.rem(lax.rem(other, 2) + at_c, 2)
            )

            @pl.when(other != me)
            def _():
                pltpu.make_async_remote_copy(
                    src_ref=part.at[other], dst_ref=landed.at[lax.rem(place + N_PT - 1, N_PT)],
                    send_sem=y_send, recv_sem=y_recv, device_id={"pt": other}, device_id_type=MESH,
                ).start()

            return carry

        lax.fori_loop(0, N_PT // 2, step, 0)

    boxes[0].wait_recv()
    last = delay(0, [jnp.zeros((HELD, LANES), BF16)] * 2)
    spill = jnp.zeros((VARS, 2 * LANES), F32)
    for m in range(BLOCKS):
        whole = product(m, 0, min(m + 1, 4))
        zmat[m, 0] = whole[:, :LANES]
        zmat[m, 1] = whole[:, LANES:]
        if m < 4:
            spill = finish(m, spill)
        if m == 3:
            hand_out(0)

    boxes[1].wait_recv()
    delay(1, last)
    for m in range(4, BLOCKS):
        rest = product(m, 4, m + 1)
        zmat[m, 0] += rest[:, :LANES]
        zmat[m, 1] += rest[:, LANES:]
        spill = finish(m, spill)
    hand_out(1)
    mine = part[me]
    parts = pltpu.make_async_remote_copy(
        src_ref=part.at[pl.ds(0, N_PT - 1)], dst_ref=landed, send_sem=y_send, recv_sem=y_recv,
        device_id=sibling, device_id_type=MESH,
    )
    for copy in boxes:
        copy.wait_send()
    parts.wait_recv()
    mine = mine + jnp.sum(landed[...], axis=0)
    for q in range(4):
        out_ref[8 * (q // 2) : 8 * (q // 2) + 8, q % 2, :] = mine[:, 32 * q : 32 * q + 32]
    parts.wait_send()


def on_device(green_tensor, moment, slip_rate, owner_shard, point_slot, live_counts):
    hbm = pl.BlockSpec(memory_space=pl.ANY)
    vmem = pl.BlockSpec(memory_space=pltpu.VMEM)
    dma = pltpu.SemaphoreType.DMA
    length = slip_rate.shape[2]
    return pl.pallas_call(
        kernel,
        out_shape=jax.ShapeDtypeStruct((VARS, 2, 32), F32),
        in_specs=[hbm] * 5 + [pl.BlockSpec(memory_space=pltpu.SMEM)],
        out_specs=vmem,
        scratch_shapes=[
            pltpu.VMEM((VARS, HELD, length), BF16),
            pltpu.VMEM((96, length), BF16),
            pltpu.VMEM(moment.shape, BF16),
            pltpu.SMEM((1, HELD), jnp.int32),
            pltpu.SMEM((HELD,), jnp.int32),
            pltpu.VMEM((LANES, LANES), F32),
            pltpu.VMEM((HELD, 16, LANES), BF16),
            pltpu.VMEM((N_PT, 1, LANES), jnp.int32),
            pltpu.VMEM((N_PT, 1, LANES), jnp.int32),
            pltpu.SMEM((N_PT, 1, LANES), jnp.int32),
            pltpu.SMEM((HELD,), jnp.int32),
            pltpu.SMEM((HELD,), jnp.int32),
            pltpu.VMEM((HELD, 16, LANES), F32),
            pltpu.VMEM((2, N_PT - 1, 16, LANES), BF16),
            pltpu.VMEM((N_PT + 1, 16, LANES), BF16),
            pltpu.VMEM((N_PT + 1, 16, LANES), BF16),
            pltpu.VMEM((HELD * 8, LANES), F32),
            pltpu.VMEM((VARS * 16, 256 * BLOCKS), BF16),
            pltpu.VMEM((256 * BLOCKS, 2 * LANES), BF16),
            pltpu.VMEM((BLOCKS, 2, VARS * 16, LANES), F32),
            pltpu.VMEM((N_PT, 8, LANES), F32),
            pltpu.VMEM((N_PT - 1, 8, LANES), F32),
            dma, dma, dma((3,)), dma, dma((N_VAR - 1,)), dma((N_VAR - 1,)), dma, dma, dma((2,)), dma((2,)), dma, dma,
        ],
        compiler_params=pltpu.CompilerParams(
            collective_id=0, has_side_effects=True, vmem_limit_bytes=60 * 1024 * 1024
        ),
        name="synthesis",
    )(slip_rate, green_tensor.reshape(96, length), moment, owner_shard.reshape(1, HELD), point_slot, live_counts)


def solution(mesh):
    in_specs = (
        P(None, None, ("pt", "var"), None),
        P(None, ("pt", "var")),
        P("var", "pt", None),
        P("pt", None),
        P("pt"),
        P("pt"),
    )
    out_specs = P("var", None, "pt")
    return jax.shard_map(on_device, mesh=mesh, in_specs=in_specs, out_specs=out_specs, check_vma=False)
```

time: 33.4 us -> 28.2 us (0.84)
  local copies, waits for them, and re-layouts: 4.17 us -> 1.32 us
  Pallas kernels: 28.3 us -> 25.8 us
    pallas_call x1, Pallas kernels: 28.3 us -> 25.8 us  [on_device(): pl.pallas_call(kernel, out_shape=jax.ShapeDtypeStruct((VARS, 2, 32), F32)...]
    unnamed x11 -> x1, local copies, waits for them, and re-layouts: 3.48 us -> 1.32 us
    transpose x1 -> x0, local copies, waits for them, and re-layouts: 0.61 us -> none  [on_device(): packed.reshape(8, 2, 2, 32).transpose(1, 0, 2, 3).reshape(VARS, 2, 32)]
where the time goes in v2:
time: 28.2 us; the launch traced here: 27.8 us
  Pallas kernels  25.8 us (91%)
  local copies, waits for them, and re-layouts  1.32 us (5%)
  between operations  0.66 us (2%)
    pallas_call x1, Pallas kernels, on_device(): pl.pallas_call(kernel, out_shape=jax.ShapeDtypeStruct((VARS, 2, 32), F32)...  25.8 us
    unnamed x1, local copies, waits for them, and re-layouts  1.32 us

profile of v2, /device:TPU:1, one launch (start us, length us, event | category | flops | bytes accessed | tf_op | source)
XLA Modules:
  0.0 27.8 jit_solution(15240888068061297742)
XLA Ops:
  0.7 25.8 %synthesis.1 = f32[16,2,32]{2,1,0:T(2,128)} custom-call(bf16[16,32,1024]{2,1,0:T(8,128)(2,1)} %slip_hbm.1, bf16[96,1024]{1,0:T(8,128)(2,1)} %bitcast.2, bf16[6,8]{1,0:T(8,128)(2,1)} %moment_hbm.1, s32[1,32]{1,0:T(1,128)} %bitcast.3, s32[32]{0:T(128)} %slot_hbm.1, s32[1]{0:T(128)S(6)} %copy.8.live_ref), custom_call_target="tpu_custom_call" | custom-call | tf_op jit(solution)/shard_map/synthesis/pallas_call | solution.py:335
  26.5 1.3 %copy.9 = f32[16,2,32]{2,1,0:T(2,128)} copy(f32[16,2,32]{2,1,0:T(2,128)} %synthesis.1) | data formatting | bytes 8192

commit v3 on v2

--- a/solution.py
+++ b/solution.py
@@ -19,28 +19,22 @@
 MESH = pl.DeviceIdType.MESH
 
 
-def each_offset(body):
-    def odd(q):
-        return 1 + 2 * lax.rem(q, 2)
-
-    def run(count, pair):
-        def step(i, carry):
-            dx, dy = pair(lax.div(i, 2))
-            body(dx, dy, lax.rem(i, 2))
-            return carry
-
-        lax.fori_loop(0, count, step, 0)
-
-    run(2, lambda q: (2, 2))
-    run(8, lambda q: (2 + lax.div(q, 2) * (odd(q) - 2), odd(q) + lax.div(q, 2) * (2 - odd(q))))
-    run(8, lambda q: (1 + 2 * lax.div(q, 2), odd(q)))
-    run(4, lambda q: (2 * lax.rem(q, 2), 2 - 2 * lax.rem(q, 2)))
-    run(8, lambda q: (lax.div(q, 2) * odd(q), (1 - lax.div(q, 2)) * odd(q)))
-    body(0, 0, 1)
+def offsets():
+    every = [(dx, dy, dc) for dx in range(4) for dy in range(4) for dc in range(2)]
+    return sorted(every[1:], key=lambda d: -(min(d[0], 4 - d[0]) + min(d[1], 4 - d[1])))
+
+
+def each_offset(body, near_first=False):
+    for dx, dy, dc in reversed(offsets()) if near_first else offsets():
+        body(dx, dy, dc)
 
 
 def code(dx, dy, dc):
-    return lax.rem(8 * dx + 2 * dy + dc + N_PT - 1, N_PT)
+    return (8 * dx + 2 * dy + dc + N_PT - 1) % N_PT
+
+
+def rank_of(level):
+    return jnp.where(level == 2, 3, jnp.where(level == 3, 2, level))
 
 
 def request_table(owner_ref, slot_ref):
@@ -59,14 +53,18 @@
     slip_hbm, green_hbm, moment_hbm, owner_hbm, slot_hbm, live_ref, out_ref,
     slip, green, moment, owner_ref, slot_ref, fold, field, ask, asked_v, asked, pick_s, second_s, field32, outbox, inbox_0, inbox_1,
     gathered, xmat, gmat, zmat, part, landed,
-    slip_sem, green_sem, small_sem, ask_sem, z_send, z_recv, q_send, q_recv, g_send, g_recv, y_send, y_recv,
+    slip_sem, green_sem, small_sem, ask_sem, z_go, z_send, z_recv, q_send, q_recv, g_send, g_recv, y_send, y_recv,
 ):
     me = lax.axis_index("pt")
     level = lax.axis_index("var")
     at_x, at_y, at_c = lax.div(me, 8), lax.rem(lax.div(me, 2), 4), lax.rem(me, 2)
 
+    xs = [lax.rem(at_x + d, 4) for d in range(4)]
+    ys = [lax.rem(at_y + d, 4) for d in range(4)]
+    cs = [at_c, 1 - at_c]
+
     def peer(dx, dy, dc):
-        return 8 * lax.rem(at_x + dx, 4) + 2 * lax.rem(at_y + dy, 4) + lax.rem(at_c + dc, 2)
+        return 8 * xs[dx] + 2 * ys[dy] + cs[dc]
 
     def above(d):
         return {"var": lax.rem(level + d, N_VAR)}
@@ -92,8 +90,13 @@
         pl.semaphore_signal(barrier, inc=1, device_id={"pt": peer(dx, dy, dc)}, device_id_type=MESH)
 
     each_offset(greet)
+    rank = rank_of(level)
+    first = [rank < rank_of(lax.rem(level + d, N_VAR)) for d in range(N_VAR)]
     for d in range(1, N_VAR):
-        pl.semaphore_signal(barrier, inc=1, device_id=above(d), device_id_type=MESH)
+
+        @pl.when(first[d])
+        def _():
+            pl.semaphore_signal(barrier, inc=1, device_id=above(d), device_id_type=MESH)
 
     for one in small:
         one.wait()
@@ -129,7 +132,12 @@
         one = jnp.concatenate([fold[pl.ds(p, 8, stride=OWN), :], fold[pl.ds(64 + p, 8, stride=OWN), :]], axis=0)
         field[level * OWN + p] = one.astype(BF16)
 
-    pl.semaphore_wait(barrier, N_PT - 1 + N_VAR - 1)
+    pl.semaphore_wait(barrier, N_PT - 1 + rank)
+    for d in range(1, N_VAR):
+
+        @pl.when(jnp.logical_not(first[d]))
+        def _():
+            pl.semaphore_signal(z_go.at[N_VAR - 1 - d], inc=1, device_id=above(d), device_id_type=MESH)
 
     def send_ask(dx, dy, dc):
         other = peer(dx, dy, dc)
@@ -147,8 +155,11 @@
         )
         for d in range(1, N_VAR)
     ]
-    for copy in spread:
-        copy.start()
+    for d in range(1, N_VAR):
+
+        @pl.when(jnp.logical_not(first[d]))
+        def _():
+            spread[d - 1].start()
 
     slip_copy.wait()
     lane16 = lax.broadcasted_iota(jnp.int32, (16, LANES), 1) // 32
@@ -172,6 +183,13 @@
 
     lax.fori_loop(0, 4, turn, 0)
 
+    for d in range(1, N_VAR):
+
+        @pl.when(first[d])
+        def _():
+            pl.semaphore_wait(z_go.at[d - 1], 1)
+            spread[d - 1].start()
+
     everyone = pltpu.make_async_remote_copy(
         src_ref=ask.at[pl.ds(0, N_PT - 1)], dst_ref=asked_v.at[pl.ds(0, N_PT - 1)], send_sem=q_send, recv_sem=q_recv,
         device_id=sibling, device_id_type=MESH,
@@ -199,7 +217,7 @@
 
         def serve(dx, dy, dc):
             place = code(dx, dy, dc)
-            outbox[half, place] = answer(code(lax.rem(4 - dx, 4), lax.rem(4 - dy, 4), dc), half)
+            outbox[half, place] = answer(code(-dx % 4, -dy % 4, dc), half)
             pltpu.make_async_remote_copy(
                 src_ref=outbox.at[half, place], dst_ref=inbox[half].at[place],
                 send_sem=g_send.at[half], recv_sem=g_recv.at[half], device_id={"pt": peer(dx, dy, dc)},
@@ -360,10 +378,10 @@
             pltpu.VMEM((BLOCKS, 2, VARS * 16, LANES), F32),
             pltpu.VMEM((N_PT, 8, LANES), F32),
             pltpu.VMEM((N_PT - 1, 8, LANES), F32),
-            dma, dma, dma((3,)), dma, dma((N_VAR - 1,)), dma((N_VAR - 1,)), dma, dma, dma((2,)), dma((2,)), dma, dma,
+            dma, dma, dma((3,)), dma, pltpu.SemaphoreType.REGULAR((N_VAR - 1,)), dma((N_VAR - 1,)), dma((N_VAR - 1,)), dma, dma, dma((2,)), dma((2,)), dma, dma,
         ],
         compiler_params=pltpu.CompilerParams(
-            collective_id=0, has_side_effects=True, vmem_limit_bytes=60 * 1024 * 1024
+            collective_id=0, has_side_effects=True, vmem_limit_bytes=55168 * 1024
         ),
         name="synthesis",
     )(slip_rate, green_tensor.reshape(96, length), moment, owner_shard.reshape(1, HELD), point_slot, live_counts)

time: 28.2 us -> 26.3 us (0.933); the launches traced: 27.8 us -> 26.2 us
  Pallas kernels: 25.8 us -> 24.2 us
    pallas_call x1, Pallas kernels: 25.8 us -> 24.2 us  [on_device(): pl.pallas_call(kernel, out_shape=jax.ShapeDtypeStruct((VARS, 2, 32), F32)...]
    unnamed x1 -> x7, local copies, waits for them, and re-layouts: 1.32 us -> 1.27 us
where the time goes in v3:
time: 26.3 us; the launch traced here: 26.2 us
  Pallas kernels  24.2 us (92%)
  local copies, waits for them, and re-layouts  1.27 us (5%)
  between operations  0.69 us (3%)
    pallas_call x1, Pallas kernels, on_device(): pl.pallas_call(kernel, out_shape=jax.ShapeDtypeStruct((VARS, 2, 32), F32)...  24.2 us
    unnamed x7, local copies, waits for them, and re-layouts  1.27 us

profile of v3, /device:TPU:1, one launch (start us, length us, event | category | flops | bytes accessed | tf_op | source)
XLA Modules:
  0.0 26.2 jit_solution(12240201133499636201)
XLA Ops:
  0.7 0.0 copy-start
  0.7 0.0 copy-start.1
  0.7 0.0 copy-start.2
  0.7 0.7 %copy-done = bf16[6,8]{1,0:T(8,128)(2,1)S(1)} copy-done((bf16[6,8]{1,0:T(8,128)(2,1)S(1)}, bf16[6,8]{1,0:T(8,128)(2,1)}, u32[]{:S(2)}) %copy-start) | copy-done | bytes 120
  1.3 0.0 copy-done.1
  1.3 0.0 copy-done.2
  1.3 24.2 %synthesis.1 = f32[16,2,32]{2,1,0:T(2,128)S(1)} custom-call(bf16[16,32,1024]{2,1,0:T(8,128)(2,1)} %slip_hbm.1, bf16[96,1024]{1,0:T(8,128)(2,1)} %bitcast.3, bf16[6,8]{1,0:T(8,128)(2,1)S(1)} %copy-done, s32[1,32]{1,0:T(1,128)S(1)} %bitcast.2, s32[32]{0:T(128)S(1)} %copy-done.2, s32[1]{0:T(128)S(6)} %copy.8.live_ref), custom_call_target="tpu_custom_call" | custom-call | tf_op jit(solution)/shard_map/synthesis/pallas_call | solution.py:353
  25.6 0.6 %copy.9 = f32[16,2,32]{2,1,0:T(2,128)} copy(f32[16,2,32]{2,1,0:T(2,128)S(1)} %synthesis.1) | data formatting | bytes 8192
Async XLA Ops:
  0.7 0.7 %copy-start = (bf16[6,8]{1,0:T(8,128)(2,1)S(1)}, bf16[6,8]{1,0:T(8,128)(2,1)}, u32[]{:S(2)}) copy-start(bf16[6,8]{1,0:T(8,128)(2,1)} %moment_hbm.1) | copy-start | bytes 292
  0.7 0.7 %copy-start.1 = (s32[32,1]{0,1:T(1,128)S(1)}, s32[32,1]{0,1:T(1,128)}, u32[]{:S(2)}) copy-start(s32[32,1]{0,1:T(1,128)} %param.9) | copy-start | bytes 388
  0.7 0.7 %copy-start.2 = (s32[32]{0:T(128)S(1)}, s32[32]{0:T(128)}, u32[]{:S(2)}) copy-start(s32[32]{0:T(128)} %slot_hbm.1) | copy-start | bytes 388

commit v4 on v3

--- a/solution.py
+++ b/solution.py
@@ -346,10 +346,14 @@
 
 
 def on_device(green_tensor, moment, slip_rate, owner_shard, point_slot, live_counts):
-    hbm = pl.BlockSpec(memory_space=pl.ANY)
+    hbm = pl.BlockSpec(memory_space=pltpu.HBM)
     vmem = pl.BlockSpec(memory_space=pltpu.VMEM)
     dma = pltpu.SemaphoreType.DMA
     length = slip_rate.shape[2]
+    in_hbm = [
+        pltpu.with_memory_space_constraint(a, pltpu.HBM)
+        for a in (slip_rate, green_tensor.reshape(96, length), moment, owner_shard.reshape(1, HELD), point_slot)
+    ]
     return pl.pallas_call(
         kernel,
         out_shape=jax.ShapeDtypeStruct((VARS, 2, 32), F32),
@@ -381,10 +385,10 @@
             dma, dma, dma((3,)), dma, pltpu.SemaphoreType.REGULAR((N_VAR - 1,)), dma((N_VAR - 1,)), dma((N_VAR - 1,)), dma, dma, dma((2,)), dma((2,)), dma, dma,
         ],
         compiler_params=pltpu.CompilerParams(
-            collective_id=0, has_side_effects=True, vmem_limit_bytes=55168 * 1024
+            collective_id=0, has_side_effects=True, vmem_limit_bytes=32 * 1024 * 1024
         ),
         name="synthesis",
-    )(slip_rate, green_tensor.reshape(96, length), moment, owner_shard.reshape(1, HELD), point_slot, live_counts)
+    )(*in_hbm, live_counts)
 
 
 def solution(mesh):

time: 26.3 us -> 25.7 us (0.977)
  local copies, waits for them, and re-layouts: 1.27 us -> 0.61 us
    unnamed x7 -> x1, local copies, waits for them, and re-layouts: 1.27 us -> 0.61 us
where the time goes in v4:
time: 25.7 us; the launch traced here: 25.6 us
  Pallas kernels  24.3 us (95%)
  between operations  0.66 us (3%)
  local copies, waits for them, and re-layouts  0.61 us (2%)
    pallas_call x1, Pallas kernels, on_device(): pl.pallas_call(kernel, out_shape=jax.ShapeDtypeStruct((VARS, 2, 32), F32)...  24.3 us
    unnamed x1, local copies, waits for them, and re-layouts  0.61 us

profile of v4, /device:TPU:1, one launch (start us, length us, event | category | flops | bytes accessed | tf_op | source)
XLA Modules:
  0.0 25.6 jit_solution(6801511011273484638)
XLA Ops:
  0.7 24.3 %synthesis.1 = f32[16,2,32]{2,1,0:T(2,128)S(1)} custom-call(bf16[16,32,1024]{2,1,0:T(8,128)(2,1)} %slip_hbm.1, bf16[96,1024]{1,0:T(8,128)(2,1)} %bitcast.2, bf16[6,8]{1,0:T(8,128)(2,1)} %moment_hbm.1, s32[1,32]{1,0:T(1,128)} %bitcast.3, s32[32]{0:T(128)} %slot_hbm.1, s32[1]{0:T(128)S(6)} %copy.8.live_ref), custom_call_target="tpu_custom_call" | custom-call | tf_op jit(solution)/shard_map/synthesis/pallas_call | solution.py:357
  25.0 0.6 %copy.9 = f32[16,2,32]{2,1,0:T(2,128)} copy(f32[16,2,32]{2,1,0:T(2,128)S(1)} %synthesis.1) | data formatting | bytes 8192

commit v5 on v4

--- a/solution.py
+++ b/solution.py
@@ -37,21 +37,24 @@
     return jnp.where(level == 2, 3, jnp.where(level == 3, 2, level))
 
 
-def request_table(owner_ref, slot_ref):
+def request_table(owner_ref, slot_ref, at_x, at_y, at_c):
     row = lax.broadcasted_iota(jnp.int32, (N_PT, LANES), 0)
     lane = lax.broadcasted_iota(jnp.int32, (N_PT, LANES), 1)
+    dx = (row // 8 + 4 - at_x) % 4
+    dy = (row // 2 + 4 - at_y) % 4
+    dc = (row + at_c) % 2
+    free = 2 * ((8 * dx + 2 * dy + dc + N_PT - 1) % N_PT)
     table = jnp.zeros((N_PT, LANES), jnp.int32)
-    count = jnp.zeros((N_PT, LANES), jnp.int32)
     for r in range(HELD):
         hit = row == owner_ref[0, r]
-        table = jnp.where(hit & (lane == count), slot_ref[r], table)
-        count = count + hit.astype(jnp.int32)
+        table = jnp.where(hit & (lane == free), slot_ref[r], table)
+        free = free + hit.astype(jnp.int32)
     return table
 
 
 def kernel(
     slip_hbm, green_hbm, moment_hbm, owner_hbm, slot_hbm, live_ref, out_ref,
-    slip, green, moment, owner_ref, slot_ref, fold, field, ask, asked_v, asked, pick_s, second_s, field32, outbox, inbox_0, inbox_1,
+    slip, green, moment, owner_ref, slot_ref, fold, field, ask, asked_v, compact, asked, pick_s, second_s, outbox, inbox_0, inbox_1,
     gathered, xmat, gmat, zmat, part, landed,
     slip_sem, green_sem, small_sem, ask_sem, z_go, z_send, z_recv, q_send, q_recv, g_send, g_recv, y_send, y_recv,
 ):
@@ -100,7 +103,7 @@
 
     for one in small:
         one.wait()
-    table = request_table(owner_ref, slot_ref)
+    table = request_table(owner_ref, slot_ref, at_x, at_y, at_c)
     for o in range(N_PT):
         ask[o] = table[o : o + 1, :]
     seen = jnp.int32(0)
@@ -195,7 +198,8 @@
         device_id=sibling, device_id_type=MESH,
     )
     everyone.wait_recv()
-    to_scalar = pltpu.make_async_copy(asked_v, asked, ask_sem)
+    compact[...] = jnp.sum(asked_v[...], axis=0)
+    to_scalar = pltpu.make_async_copy(compact, asked, ask_sem)
     to_scalar.start()
     for d in range(1, N_VAR):
         source = lax.rem(level + (N_VAR - d), N_VAR)
@@ -204,29 +208,33 @@
             send_sem=z_send.at[d - 1], recv_sem=z_recv.at[d - 1], device_id=above(d), device_id_type=MESH,
         ).wait_recv()
 
-    for p in range(HELD):
-        field32[p] = field[p].astype(F32)
     to_scalar.wait()
 
-    def answer(where, half):
-        rows = [field32[asked[where, 0, slot], 8 * half : 8 * half + 8, :] for slot in range(2)]
-        return jnp.concatenate(rows, axis=0).astype(BF16)
+    def answer(where):
+        points = [field[asked[0, 2 * where + slot]].astype(F32) for slot in range(2)]
+        return [
+            jnp.concatenate([point[8 * half : 8 * half + 8] for point in points], axis=0).astype(BF16)
+            for half in range(2)
+        ]
 
     inbox = [inbox_0, inbox_1]
+
+    def send_box(half, dx, dy, dc):
+        place = code(dx, dy, dc)
+        pltpu.make_async_remote_copy(
+            src_ref=outbox.at[half, place], dst_ref=inbox[half].at[place], send_sem=g_send.at[half],
+            recv_sem=g_recv.at[half], device_id={"pt": peer(dx, dy, dc)}, device_id_type=MESH,
+        ).start()
+
+    def serve(dx, dy, dc):
+        place = code(dx, dy, dc)
+        outbox[0, place], outbox[1, place] = answer(code(-dx % 4, -dy % 4, dc))
+        send_box(0, dx, dy, dc)
+
+    each_offset(serve)
+    each_offset(functools.partial(send_box, 1))
+    inbox_0[N_PT - 1], inbox_1[N_PT - 1] = answer(N_PT - 1)
     for half in range(2):
-
-        def serve(dx, dy, dc):
-            place = code(dx, dy, dc)
-            outbox[half, place] = answer(code(-dx % 4, -dy % 4, dc), half)
-            pltpu.make_async_remote_copy(
-                src_ref=outbox.at[half, place], dst_ref=inbox[half].at[place],
-                send_sem=g_send.at[half], recv_sem=g_recv.at[half], device_id={"pt": peer(dx, dy, dc)},
-                device_id_type=MESH,
-            ).start()
-
-        each_offset(serve)
-    for half in range(2):
-        inbox[half][N_PT - 1] = answer(N_PT - 1, half)
         inbox[half][N_PT] = jnp.zeros((16, LANES), BF16)
     boxes = [
         pltpu.make_async_remote_copy(
@@ -291,25 +299,22 @@
             part[4 * m + t] = mixed
         return spill
 
-    def hand_out(half):
-        def step(i, carry):
-            other = (N_PT // 2) * half + lax.rem(me + i, N_PT // 2)
-            place = (
-                8 * lax.rem(lax.div(other, 8) + 4 - at_x, 4)
-                + 2 * lax.rem(lax.rem(lax.div(other, 2), 4) + 4 - at_y, 4)
-                + lax.rem(lax.rem(other, 2) + at_c, 2)
-            )
-
-            @pl.when(other != me)
-            def _():
-                pltpu.make_async_remote_copy(
-                    src_ref=part.at[other], dst_ref=landed.at[lax.rem(place + N_PT - 1, N_PT)],
-                    send_sem=y_send, recv_sem=y_recv, device_id={"pt": other}, device_id_type=MESH,
-                ).start()
-
-            return carry
-
-        lax.fori_loop(0, N_PT // 2, step, 0)
+    def hand_out(x):
+        base = 8 * lax.rem(x + 4 - at_x, 4)
+
+        def give(dy, dc):
+            other = 8 * x + 2 * ys[dy] + cs[dc]
+            pltpu.make_async_remote_copy(
+                src_ref=part.at[other], dst_ref=landed.at[base + 2 * dy + dc - 1], send_sem=y_send, recv_sem=y_recv,
+                device_id={"pt": other}, device_id_type=MESH,
+            ).start()
+
+        for dy, dc in [(2, 0), (2, 1), (1, 0), (1, 1), (3, 0), (3, 1), (0, 1)]:
+            give(dy, dc)
+
+        @pl.when(base > 0)
+        def _():
+            give(0, 0)
 
     boxes[0].wait_recv()
     last = delay(0, [jnp.zeros((HELD, LANES), BF16)] * 2)
@@ -320,8 +325,8 @@
         zmat[m, 1] = whole[:, LANES:]
         if m < 4:
             spill = finish(m, spill)
-        if m == 3:
-            hand_out(0)
+        if m in (1, 3):
+            hand_out(m // 2)
 
     boxes[1].wait_recv()
     delay(1, last)
@@ -330,7 +335,8 @@
         zmat[m, 0] += rest[:, :LANES]
         zmat[m, 1] += rest[:, LANES:]
         spill = finish(m, spill)
-    hand_out(1)
+    hand_out(3)
+    hand_out(2)
     mine = part[me]
     parts = pltpu.make_async_remote_copy(
         src_ref=part.at[pl.ds(0, N_PT - 1)], dst_ref=landed, send_sem=y_send, recv_sem=y_recv,
@@ -369,10 +375,10 @@
             pltpu.VMEM((HELD, 16, LANES), BF16),
             pltpu.VMEM((N_PT, 1, LANES), jnp.int32),
             pltpu.VMEM((N_PT, 1, LANES), jnp.int32),
-            pltpu.SMEM((N_PT, 1, LANES), jnp.int32),
+            pltpu.VMEM((1, LANES), jnp.int32),
+            pltpu.SMEM((1, LANES), jnp.int32),
             pltpu.SMEM((HELD,), jnp.int32),
             pltpu.SMEM((HELD,), jnp.int32),
-            pltpu.VMEM((HELD, 16, LANES), F32),
             pltpu.VMEM((2, N_PT - 1, 16, LANES), BF16),
             pltpu.VMEM((N_PT + 1, 16, LANES), BF16),
             pltpu.VMEM((N_PT + 1, 16, LANES), BF16),

time: 25.7 us -> 25.7 us (level)
  no operation moved by 1% of the time
where the time goes in v5:
time: 25.7 us; the launch traced here: 25.5 us
  Pallas kernels  24.3 us (95%)
  between operations  0.66 us (3%)
  local copies, waits for them, and re-layouts  0.61 us (2%)
    pallas_call x1, Pallas kernels, on_device(): pl.pallas_call(kernel, out_shape=jax.ShapeDtypeStruct((VARS, 2, 32), F32)...  24.3 us
    unnamed x1, local copies, waits for them, and re-layouts  0.61 us

profile of v5, /device:TPU:1, one launch (start us, length us, event | category | flops | bytes accessed | tf_op | source)
XLA Modules:
  0.0 25.5 jit_solution(4553300018008963062)
XLA Ops:
  0.7 24.3 %synthesis.1 = f32[16,2,32]{2,1,0:T(2,128)S(1)} custom-call(bf16[16,32,1024]{2,1,0:T(8,128)(2,1)} %slip_hbm.1, bf16[96,1024]{1,0:T(8,128)(2,1)} %bitcast.2, bf16[6,8]{1,0:T(8,128)(2,1)} %moment_hbm.1, s32[1,32]{1,0:T(1,128)} %bitcast.3, s32[32]{0:T(128)} %slot_hbm.1, s32[1]{0:T(128)S(6)} %copy.8.live_ref), custom_call_target="tpu_custom_call" | custom-call | tf_op jit(solution)/shard_map/synthesis/pallas_call | solution.py:363
  24.9 0.6 %copy.9 = f32[16,2,32]{2,1,0:T(2,128)} copy(f32[16,2,32]{2,1,0:T(2,128)S(1)} %synthesis.1) | data formatting | bytes 8192

commit v6 on v5

--- a/solution.py
+++ b/solution.py
@@ -54,7 +54,7 @@
 
 def kernel(
     slip_hbm, green_hbm, moment_hbm, owner_hbm, slot_hbm, live_ref, out_ref,
-    slip, green, moment, owner_ref, slot_ref, fold, field, ask, asked_v, compact, asked, pick_s, second_s, outbox, inbox_0, inbox_1,
+    slip, green, moment, owner_ref, slot_ref, fold, field_0, field_1, ask, asked_v, compact, asked, pick_s, second_s, outbox, inbox_0, inbox_1,
     gathered, xmat, gmat, zmat, part, landed,
     slip_sem, green_sem, small_sem, ask_sem, z_go, z_send, z_recv, q_send, q_recv, g_send, g_recv, y_send, y_recv,
 ):
@@ -72,6 +72,7 @@
     def above(d):
         return {"var": lax.rem(level + d, N_VAR)}
 
+    field = [field_0, field_1]
     sibling = {"pt": peer(0, 0, 1)}
 
     slip_copy = pltpu.make_async_copy(slip_hbm, slip, slip_sem)
@@ -131,9 +132,10 @@
         for h in range(2):
             row = OWN * (8 * (m // 4) + 4 * h + m % 4)
             fold[row : row + OWN, :] = total[OWN * h : OWN * h + OWN]
-    for p in range(OWN):
-        one = jnp.concatenate([fold[pl.ds(p, 8, stride=OWN), :], fold[pl.ds(64 + p, 8, stride=OWN), :]], axis=0)
-        field[level * OWN + p] = one.astype(BF16)
+    for half in range(2):
+        for q in range(OWN // 2):
+            two = [fold[pl.ds(64 * half + 2 * q + i, 8, stride=OWN), :] for i in range(2)]
+            field[half][level * (OWN // 2) + q] = jnp.concatenate(two, axis=0).astype(BF16)
 
     pl.semaphore_wait(barrier, N_PT - 1 + rank)
     for d in range(1, N_VAR):
@@ -141,6 +143,20 @@
         @pl.when(jnp.logical_not(first[d]))
         def _():
             pl.semaphore_signal(z_go.at[N_VAR - 1 - d], inc=1, device_id=above(d), device_id_type=MESH)
+
+    def spread(half, d):
+        mine = field[half].at[pl.ds(level * (OWN // 2), OWN // 2)]
+        return pltpu.make_async_remote_copy(
+            src_ref=mine, dst_ref=mine, send_sem=z_send.at[half, d - 1], recv_sem=z_recv.at[half, d - 1],
+            device_id=above(d), device_id_type=MESH,
+        )
+
+    for half in range(2):
+        for d in (2, 1, 3):
+
+            @pl.when(jnp.logical_not(first[d]))
+            def _():
+                spread(half, d).start()
 
     def send_ask(dx, dy, dc):
         other = peer(dx, dy, dc)
@@ -151,19 +167,6 @@
 
     each_offset(send_ask)
     asked_v[N_PT - 1] = ask[me]
-    spread = [
-        pltpu.make_async_remote_copy(
-            src_ref=field.at[pl.ds(level * OWN, OWN)], dst_ref=field.at[pl.ds(level * OWN, OWN)],
-            send_sem=z_send.at[d - 1], recv_sem=z_recv.at[d - 1], device_id=above(d), device_id_type=MESH,
-        )
-        for d in range(1, N_VAR)
-    ]
-    for d in range(1, N_VAR):
-
-        @pl.when(jnp.logical_not(first[d]))
-        def _():
-            spread[d - 1].start()
-
     slip_copy.wait()
     lane16 = lax.broadcasted_iota(jnp.int32, (16, LANES), 1) // 32
 
@@ -191,7 +194,8 @@
         @pl.when(first[d])
         def _():
             pl.semaphore_wait(z_go.at[d - 1], 1)
-            spread[d - 1].start()
+            spread(0, d).start()
+            spread(1, d).start()
 
     everyone = pltpu.make_async_remote_copy(
         src_ref=ask.at[pl.ds(0, N_PT - 1)], dst_ref=asked_v.at[pl.ds(0, N_PT - 1)], send_sem=q_send, recv_sem=q_recv,
@@ -201,40 +205,35 @@
     compact[...] = jnp.sum(asked_v[...], axis=0)
     to_scalar = pltpu.make_async_copy(compact, asked, ask_sem)
     to_scalar.start()
-    for d in range(1, N_VAR):
-        source = lax.rem(level + (N_VAR - d), N_VAR)
-        pltpu.make_async_remote_copy(
-            src_ref=field.at[pl.ds(level * OWN, OWN)], dst_ref=field.at[pl.ds(source * OWN, OWN)],
-            send_sem=z_send.at[d - 1], recv_sem=z_recv.at[d - 1], device_id=above(d), device_id_type=MESH,
-        ).wait_recv()
-
     to_scalar.wait()
 
-    def answer(where):
-        points = [field[asked[0, 2 * where + slot]].astype(F32) for slot in range(2)]
-        return [
-            jnp.concatenate([point[8 * half : 8 * half + 8] for point in points], axis=0).astype(BF16)
-            for half in range(2)
-        ]
+    def answer(half, where):
+        rows = []
+        for slot in range(2):
+            point = asked[0, 2 * where + slot]
+            two = field[half][lax.div(point, 2)].astype(F32)
+            rows.append(jnp.where(lax.rem(point, 2) == 1, two[8:], two[:8]))
+        return jnp.concatenate(rows, axis=0).astype(BF16)
 
     inbox = [inbox_0, inbox_1]
-
-    def send_box(half, dx, dy, dc):
-        place = code(dx, dy, dc)
-        pltpu.make_async_remote_copy(
-            src_ref=outbox.at[half, place], dst_ref=inbox[half].at[place], send_sem=g_send.at[half],
-            recv_sem=g_recv.at[half], device_id={"pt": peer(dx, dy, dc)}, device_id_type=MESH,
-        ).start()
-
-    def serve(dx, dy, dc):
-        place = code(dx, dy, dc)
-        outbox[0, place], outbox[1, place] = answer(code(-dx % 4, -dy % 4, dc))
-        send_box(0, dx, dy, dc)
-
-    each_offset(serve)
-    each_offset(functools.partial(send_box, 1))
-    inbox_0[N_PT - 1], inbox_1[N_PT - 1] = answer(N_PT - 1)
     for half in range(2):
+        for d in range(1, N_VAR):
+            theirs = field[half].at[pl.ds(lax.rem(level + (N_VAR - d), N_VAR) * (OWN // 2), OWN // 2)]
+            pltpu.make_async_remote_copy(
+                src_ref=theirs, dst_ref=theirs, send_sem=z_send.at[half, d - 1], recv_sem=z_recv.at[half, d - 1],
+                device_id=above(d), device_id_type=MESH,
+            ).wait_recv()
+
+        def serve(dx, dy, dc):
+            place = code(dx, dy, dc)
+            outbox[half, place] = answer(half, code(-dx % 4, -dy % 4, dc))
+            pltpu.make_async_remote_copy(
+                src_ref=outbox.at[half, place], dst_ref=inbox[half].at[place], send_sem=g_send.at[half],
+                recv_sem=g_recv.at[half], device_id={"pt": peer(dx, dy, dc)}, device_id_type=MESH,
+            ).start()
+
+        each_offset(serve)
+        inbox[half][N_PT - 1] = answer(half, N_PT - 1)
         inbox[half][N_PT] = jnp.zeros((16, LANES), BF16)
     boxes = [
         pltpu.make_async_remote_copy(
@@ -244,8 +243,9 @@
         for half in range(2)
     ]
     everyone.wait_send()
-    for copy in spread:
-        copy.wait_send()
+    for half in range(2):
+        for d in range(1, N_VAR):
+            spread(half, d).wait_send()
 
     lane32 = lax.broadcasted_iota(jnp.int32, (HELD, LANES), 1)
     wide = lax.broadcasted_iota(jnp.int32, (VARS, 2 * LANES), 1) % LANES
@@ -372,7 +372,8 @@
             pltpu.SMEM((1, HELD), jnp.int32),
             pltpu.SMEM((HELD,), jnp.int32),
             pltpu.VMEM((LANES, LANES), F32),
-            pltpu.VMEM((HELD, 16, LANES), BF16),
+            pltpu.VMEM((HELD // 2, 16, LANES), BF16),
+            pltpu.VMEM((HELD // 2, 16, LANES), BF16),
             pltpu.VMEM((N_PT, 1, LANES), jnp.int32),
             pltpu.VMEM((N_PT, 1, LANES), jnp.int32),
             pltpu.VMEM((1, LANES), jnp.int32),
@@ -388,7 +389,7 @@
             pltpu.VMEM((BLOCKS, 2, VARS * 16, LANES), F32),
             pltpu.VMEM((N_PT, 8, LANES), F32),
             pltpu.VMEM((N_PT - 1, 8, LANES), F32),
-            dma, dma, dma((3,)), dma, pltpu.SemaphoreType.REGULAR((N_VAR - 1,)), dma((N_VAR - 1,)), dma((N_VAR - 1,)), dma, dma, dma((2,)), dma((2,)), dma, dma,
+            dma, dma, dma((3,)), dma, pltpu.SemaphoreType.REGULAR((N_VAR - 1,)), dma((2, N_VAR - 1)), dma((2, N_VAR - 1)), dma, dma, dma((2,)), dma((2,)), dma, dma,
         ],
         compiler_params=pltpu.CompilerParams(
             collective_id=0, has_side_effects=True, vmem_limit_bytes=32 * 1024 * 1024

time: 25.7 us -> 25 us (0.973)
  Pallas kernels: 24.3 us -> 23.6 us
    pallas_call x1, Pallas kernels: 24.3 us -> 23.6 us  [on_device(): pl.pallas_call(kernel, out_shape=jax.ShapeDtypeStruct((VARS, 2, 32), F32)...]
where the time goes in v6:
time: 25 us; the launch traced here: 24.9 us
  Pallas kernels  23.6 us (94%)
  between operations  0.66 us (3%)
  local copies, waits for them, and re-layouts  0.61 us (2%)
    pallas_call x1, Pallas kernels, on_device(): pl.pallas_call(kernel, out_shape=jax.ShapeDtypeStruct((VARS, 2, 32), F32)...  23.6 us
    unnamed x1, local copies, waits for them, and re-layouts  0.61 us

profile of v6, /device:TPU:1, one launch (start us, length us, event | category | flops | bytes accessed | tf_op | source)
XLA Modules:
  0.0 24.9 jit_solution(500320983790161717)
XLA Ops:
  0.7 23.6 %synthesis.1 = f32[16,2,32]{2,1,0:T(2,128)S(1)} custom-call(bf16[16,32,1024]{2,1,0:T(8,128)(2,1)} %slip_hbm.1, bf16[96,1024]{1,0:T(8,128)(2,1)} %bitcast.2, bf16[6,8]{1,0:T(8,128)(2,1)} %moment_hbm.1, s32[1,32]{1,0:T(1,128)} %bitcast.3, s32[32]{0:T(128)} %slot_hbm.1, s32[1]{0:T(128)S(6)} %copy.8.live_ref), custom_call_target="tpu_custom_call" | custom-call | tf_op jit(solution)/shard_map/synthesis/pallas_call | solution.py:363
  24.3 0.6 %copy.9 = f32[16,2,32]{2,1,0:T(2,128)} copy(f32[16,2,32]{2,1,0:T(2,128)S(1)} %synthesis.1) | data formatting | bytes 8192

commit v7 on v6

--- a/solution.py
+++ b/solution.py
@@ -107,6 +107,51 @@
     table = request_table(owner_ref, slot_ref, at_x, at_y, at_c)
     for o in range(N_PT):
         ask[o] = table[o : o + 1, :]
+    green_copy.wait()
+    tall = jnp.transpose(moment[...].astype(F32))
+    tall = jnp.concatenate([tall, tall], axis=0)
+    for m in range(BLOCKS):
+        total = jnp.zeros((2 * OWN, LANES), F32)
+        for c in range(6):
+            total = total + tall[:, c : c + 1] * green[16 * c : 16 * c + 16, LANES * m : LANES * (m + 1)].astype(F32)
+        for h in range(2):
+            row = OWN * (8 * (m // 4) + 4 * h + m % 4)
+            fold[row : row + OWN, :] = total[OWN * h : OWN * h + OWN]
+    for half in range(2):
+        for q in range(OWN // 2):
+            two = [fold[pl.ds(64 * half + 2 * q + i, 8, stride=OWN), :] for i in range(2)]
+            field[half][level * (OWN // 2) + q] = jnp.concatenate(two, axis=0).astype(BF16)
+
+    pl.semaphore_wait(barrier, N_PT - 1 + rank)
+    for d in range(1, N_VAR):
+
+        @pl.when(jnp.logical_not(first[d]))
+        def _():
+            pl.semaphore_signal(z_go.at[N_VAR - 1 - d], inc=1, device_id=above(d), device_id_type=MESH)
+
+    def spread(half, d):
+        mine = field[half].at[pl.ds(level * (OWN // 2), OWN // 2)]
+        return pltpu.make_async_remote_copy(
+            src_ref=mine, dst_ref=mine, send_sem=z_send.at[half, d - 1], recv_sem=z_recv.at[half, d - 1],
+            device_id=above(d), device_id_type=MESH,
+        )
+
+    for half in range(2):
+        for d in (2, 1, 3):
+
+            @pl.when(jnp.logical_not(first[d]))
+            def _():
+                spread(half, d).start()
+
+    def send_ask(dx, dy, dc):
+        other = peer(dx, dy, dc)
+        pltpu.make_async_remote_copy(
+            src_ref=ask.at[other], dst_ref=asked_v.at[code(dx, dy, dc)], send_sem=q_send, recv_sem=q_recv,
+            device_id={"pt": other}, device_id_type=MESH,
+        ).start()
+
+    each_offset(send_ask)
+    asked_v[N_PT - 1] = ask[me]
     seen = jnp.int32(0)
     for r in range(HELD):
         owner = owner_ref[0, r]
@@ -122,51 +167,6 @@
         pick_s[r] = jnp.where(r < live_ref[0], place, N_PT)
         second_s[r] = second
 
-    green_copy.wait()
-    tall = jnp.transpose(moment[...].astype(F32))
-    tall = jnp.concatenate([tall, tall], axis=0)
-    for m in range(BLOCKS):
-        total = jnp.zeros((2 * OWN, LANES), F32)
-        for c in range(6):
-            total = total + tall[:, c : c + 1] * green[16 * c : 16 * c + 16, LANES * m : LANES * (m + 1)].astype(F32)
-        for h in range(2):
-            row = OWN * (8 * (m // 4) + 4 * h + m % 4)
-            fold[row : row + OWN, :] = total[OWN * h : OWN * h + OWN]
-    for half in range(2):
-        for q in range(OWN // 2):
-            two = [fold[pl.ds(64 * half + 2 * q + i, 8, stride=OWN), :] for i in range(2)]
-            field[half][level * (OWN // 2) + q] = jnp.concatenate(two, axis=0).astype(BF16)
-
-    pl.semaphore_wait(barrier, N_PT - 1 + rank)
-    for d in range(1, N_VAR):
-
-        @pl.when(jnp.logical_not(first[d]))
-        def _():
-            pl.semaphore_signal(z_go.at[N_VAR - 1 - d], inc=1, device_id=above(d), device_id_type=MESH)
-
-    def spread(half, d):
-        mine = field[half].at[pl.ds(level * (OWN // 2), OWN // 2)]
-        return pltpu.make_async_remote_copy(
-            src_ref=mine, dst_ref=mine, send_sem=z_send.at[half, d - 1], recv_sem=z_recv.at[half, d - 1],
-            device_id=above(d), device_id_type=MESH,
-        )
-
-    for half in range(2):
-        for d in (2, 1, 3):
-
-            @pl.when(jnp.logical_not(first[d]))
-            def _():
-                spread(half, d).start()
-
-    def send_ask(dx, dy, dc):
-        other = peer(dx, dy, dc)
-        pltpu.make_async_remote_copy(
-            src_ref=ask.at[other], dst_ref=asked_v.at[code(dx, dy, dc)], send_sem=q_send, recv_sem=q_recv,
-            device_id={"pt": other}, device_id_type=MESH,
-        ).start()
-
-    each_offset(send_ask)
-    asked_v[N_PT - 1] = ask[me]
     slip_copy.wait()
     lane16 = lax.broadcasted_iota(jnp.int32, (16, LANES), 1) // 32
 

time: 25 us -> 25 us (level)
  no operation moved by 1% of the time
where the time goes in v7:
time: 25 us; the launch traced here: 24.9 us
  Pallas kernels  23.6 us (94%)
  between operations  0.66 us (3%)
  local copies, waits for them, and re-layouts  0.61 us (2%)
    pallas_call x1, Pallas kernels, on_device(): pl.pallas_call(kernel, out_shape=jax.ShapeDtypeStruct((VARS, 2, 32), F32)...  23.6 us
    unnamed x1, local copies, waits for them, and re-layouts  0.61 us

profile of v7, /device:TPU:1, one launch (start us, length us, event | category | flops | bytes accessed | tf_op | source)
XLA Modules:
  0.0 24.9 jit_solution(6282668840160971639)
XLA Ops:
  0.7 23.6 %synthesis.1 = f32[16,2,32]{2,1,0:T(2,128)S(1)} custom-call(bf16[16,32,1024]{2,1,0:T(8,128)(2,1)} %slip_hbm.1, bf16[96,1024]{1,0:T(8,128)(2,1)} %bitcast.2, bf16[6,8]{1,0:T(8,128)(2,1)} %moment_hbm.1, s32[1,32]{1,0:T(1,128)} %bitcast.3, s32[32]{0:T(128)} %slot_hbm.1, s32[1]{0:T(128)S(6)} %copy.8.live_ref), custom_call_target="tpu_custom_call" | custom-call | tf_op jit(solution)/shard_map/synthesis/pallas_call | solution.py:363
  24.3 0.6 %copy.9 = f32[16,2,32]{2,1,0:T(2,128)} copy(f32[16,2,32]{2,1,0:T(2,128)S(1)} %synthesis.1) | data formatting | bytes 8192

commit v8 on v6

--- a/solution.py
+++ b/solution.py
@@ -83,25 +83,25 @@
             [(owner_hbm, owner_ref), (slot_hbm, slot_ref), (moment_hbm, moment)]
         )
     ]
+
+    barrier = pltpu.get_barrier_semaphore()
+
+    def greet(dx, dy, dc):
+        pl.semaphore_signal(barrier, inc=1, device_id={"pt": peer(dx, dy, dc)}, device_id_type=MESH)
+
+    each_offset(greet)
+    rank = rank_of(level)
+    first = [rank < rank_of(lax.rem(level + d, N_VAR)) for d in range(N_VAR)]
+    for d in range(1, N_VAR):
+
+        @pl.when(first[d])
+        def _():
+            pl.semaphore_signal(barrier, inc=1, device_id=above(d), device_id_type=MESH)
+
     for one in small:
         one.start()
     green_copy.start()
     slip_copy.start()
-
-    barrier = pltpu.get_barrier_semaphore()
-
-    def greet(dx, dy, dc):
-        pl.semaphore_signal(barrier, inc=1, device_id={"pt": peer(dx, dy, dc)}, device_id_type=MESH)
-
-    each_offset(greet)
-    rank = rank_of(level)
-    first = [rank < rank_of(lax.rem(level + d, N_VAR)) for d in range(N_VAR)]
-    for d in range(1, N_VAR):
-
-        @pl.when(first[d])
-        def _():
-            pl.semaphore_signal(barrier, inc=1, device_id=above(d), device_id_type=MESH)
-
     for one in small:
         one.wait()
     table = request_table(owner_ref, slot_ref, at_x, at_y, at_c)

time: 25 us -> 25 us (level)
  no operation moved by 1% of the time
where the time goes in v8:
time: 25 us; the launch traced here: 24.9 us
  Pallas kernels  23.6 us (94%)
  between operations  0.66 us (3%)
  local copies, waits for them, and re-layouts  0.61 us (2%)
    pallas_call x1, Pallas kernels, on_device(): pl.pallas_call(kernel, out_shape=jax.ShapeDtypeStruct((VARS, 2, 32), F32)...  23.6 us
    unnamed x1, local copies, waits for them, and re-layouts  0.61 us

profile of v8, /device:TPU:1, one launch (start us, length us, event | category | flops | bytes accessed | tf_op | source)
XLA Modules:
  0.0 24.9 jit_solution(14786132496904522841)
XLA Ops:
  0.7 23.6 %synthesis.1 = f32[16,2,32]{2,1,0:T(2,128)S(1)} custom-call(bf16[16,32,1024]{2,1,0:T(8,128)(2,1)} %slip_hbm.1, bf16[96,1024]{1,0:T(8,128)(2,1)} %bitcast.2, bf16[6,8]{1,0:T(8,128)(2,1)} %moment_hbm.1, s32[1,32]{1,0:T(1,128)} %bitcast.3, s32[32]{0:T(128)} %slot_hbm.1, s32[1]{0:T(128)S(6)} %copy.8.live_ref), custom_call_target="tpu_custom_call" | custom-call | tf_op jit(solution)/shard_map/synthesis/pallas_call | solution.py:363
  24.3 0.6 %copy.9 = f32[16,2,32]{2,1,0:T(2,128)} copy(f32[16,2,32]{2,1,0:T(2,128)S(1)} %synthesis.1) | data formatting | bytes 8192
